TPU v7x, 32 devices: a whole 2x2x4 slice. The times are simulated.
32 devices in a mesh: vert: 4 (over z), feat: 8 (over y, x, core).
Axes of the slice: x: 2, y: 2, z: 4, core: 2. Of those that a mesh axis runs over, the one named last changes fastest.
Arguments:
- states: bfloat16 [4, 256, 16384], P(None, 'feat', 'vert'), may hold values from -6 to 6
- depth_weight: float32 [4, 256], P(None, 'feat'), may hold values from -1 to 1
- tile_values: bfloat16 [4, 256, 128, 128], P('vert'), may hold values from -0.1875 to 0.1875
- tile_dst: int32 [4, 256], P('vert'), may hold values from 0 to 31
- tile_src: int32 [4, 256], P('vert'), may hold values from 0 to 33
- tile_count: int32 [4], P('vert'), may hold values from 64 to 256, as said below
- send_rows: int32 [4, 4, 64], P('vert'), may hold values from 0 to 4095
- weight: bfloat16 [256, 256], replicated, may hold values from -0.375 to 0.375
- bias_vec: float32 [256], P('feat'), may hold values from -3 to 3
- cotangent: bfloat16 [256, 16384], P('feat', 'vert'), may hold values from -6 to 6
Outputs:
- layer_out: bfloat16 [256, 16384], P('feat', 'vert')
- grad_states: bfloat16 [4, 256, 16384], P(None, 'feat', 'vert')
- grad_weight: float32 [256, 256], P('feat')
- grad_bias: float32 [256], P('feat')
- grad_depth: float32 [4, 256], P(None, 'feat')
Inputs may be any that keep to these rules, and one draw needn't show every extreme that they name: `tile_count`: at least 64 tiles in every partition, and exactly 256 in some partition.
All inputs are finite; a program needn't handle non-finite values.
Results may differ from a plain program's by a relative error of at most 0.024.
Values may be sent and summed in bfloat16 or wider, within the bound.
A program may use at most 64 MiB of HBM per device.

v0:
```python
import math

import jax
import jax.numpy as jnp
from jax import lax
from jax.sharding import PartitionSpec as P


def tile_forward(extended, tile_grp, dst_grp, src_grp, live_mask, row_blocks):
    picked = jnp.take(extended, src_grp, axis=1)
    products = jnp.einsum("dtc,trc->dtr", picked, tile_grp, preferred_element_type=jnp.float32)
    onehot = (
        (dst_grp[:, None] == jnp.arange(row_blocks, dtype=jnp.int32)[None, :]) & live_mask[:, None]
    ).astype(jnp.float32)
    return jnp.einsum("dtr,tn->dnr", products, onehot)


def tile_backward(grad_blocks, tile_grp, dst_grp, src_grp, live_mask, src_blocks):
    picked = jnp.take(grad_blocks, dst_grp, axis=1)
    products = jnp.einsum("dtr,trc->dtc", picked, tile_grp, preferred_element_type=jnp.float32)
    onehot = (
        (src_grp[:, None] == jnp.arange(src_blocks, dtype=jnp.int32)[None, :]) & live_mask[:, None]
    ).astype(jnp.float32)
    return jnp.einsum("dtc,ts->dsc", products, onehot)


def over_tiles(kernel, source, tile_values, tile_dst, tile_src, tile_total, out_blocks):
    capacity = tile_values.shape[0]
    live_mask = jnp.arange(capacity, dtype=jnp.int32) < tile_total
    return kernel(source, tile_values, tile_dst, tile_src, live_mask, out_blocks)


def local(
    states,
    depth_weight,
    tile_values,
    tile_dst,
    tile_src,
    tile_count,
    send_rows,
    weight,
    bias_vec,
    cotangent,
):
    channels = states.shape[1]
    row_count = states.shape[2]
    block_size = tile_values.shape[2]
    row_blocks = row_count // block_size
    my_tiles = tile_values[0]
    my_dst = tile_dst[0]
    my_src = tile_src[0]
    tile_total = tile_count[0]
    my_send = send_rows[0]
    section_count = my_send.shape[0]
    halo_width = my_send.shape[1]
    vert_count = lax.axis_size("vert")
    panel_start = lax.axis_index("feat") * channels
    src_blocks = (row_count + section_count * halo_width) // block_size
    norm_scale = 1.0 / math.sqrt(vert_count * row_count)
    weight_rows = lax.dynamic_slice_in_dim(weight, panel_start, channels, 0)
    mixed_state = jnp.sum(depth_weight[:, :, None] * states, axis=0).astype(jnp.bfloat16)
    outgoing = mixed_state[:, my_send]
    incoming = lax.all_to_all(outgoing, "vert", split_axis=1, concat_axis=1, tiled=True)
    extended = jnp.concatenate([mixed_state, incoming.reshape(channels, -1)], axis=1)
    extended = extended.reshape(channels, src_blocks, block_size)
    aggregated = over_tiles(
        tile_forward, extended, my_tiles, my_dst, my_src, tile_total, row_blocks
    )
    aggregated = aggregated.reshape(channels, row_count).astype(jnp.bfloat16)
    pre_act = lax.psum_scatter(
        lax.dot_general(
            weight_rows, aggregated, (((0,), (0,)), ((), ())), preferred_element_type=jnp.float32
        ).astype(jnp.bfloat16),
        "feat",
        scatter_dimension=0,
        tiled=True,
    ).astype(jnp.float32)
    pre_act = pre_act + bias_vec[:, None]
    sigmoid_pre = jax.nn.sigmoid(pre_act)
    layer_out = (pre_act * sigmoid_pre).astype(jnp.bfloat16)
    grad_pre = (
        cotangent.astype(jnp.float32) * sigmoid_pre * (1.0 + pre_act * (1.0 - sigmoid_pre))
    ).astype(jnp.bfloat16)
    piece = lax.all_gather(grad_pre, "feat", axis=0, tiled=True)
    agg_total = jnp.dot(weight_rows, piece, preferred_element_type=jnp.float32)
    terms_now = lax.dot_general(
        aggregated, piece, (((1,), (1,)), ((), ())), preferred_element_type=jnp.float32
    )
    grad_agg = agg_total.astype(jnp.bfloat16)
    grad_blocks = grad_agg.reshape(channels, row_blocks, block_size)
    spread_out = over_tiles(
        tile_backward, grad_blocks, my_tiles, my_dst, my_src, tile_total, src_blocks
    )
    spread_out = spread_out.reshape(channels, src_blocks * block_size)
    halo_terms = (
        spread_out[:, row_count:].astype(jnp.bfloat16).reshape(channels, section_count, halo_width)
    )
    returned = lax.all_to_all(halo_terms, "vert", split_axis=1, concat_axis=1, tiled=True)
    grad_mixed = spread_out[:, :row_count].at[:, my_send].add(returned.astype(jnp.float32))
    grad_states = (depth_weight[:, :, None] * grad_mixed[None]).astype(jnp.bfloat16)
    bias_terms = jnp.sum(grad_pre.astype(jnp.float32), axis=1)
    depth_terms = jnp.sum(states * grad_mixed[None], axis=2)
    weight_sum, bias_sum, depth_sum = lax.psum((terms_now, bias_terms, depth_terms), "vert")
    return (
        layer_out,
        grad_states,
        weight_sum * norm_scale,
        bias_sum * norm_scale,
        depth_sum * norm_scale,
    )


def solution(mesh):
    placed = (
        P(None, "feat", "vert"),
        P(None, "feat"),
        P("vert", None, None, None),
        P("vert", None),
        P("vert", None),
        P("vert"),
        P("vert", None, None),
        P(),
        P("feat"),
        P("feat", "vert"),
    )
    return jax.shard_map(
        local,
        mesh=mesh,
        in_specs=placed,
        out_specs=(
            P("feat", "vert"),
            P(None, "feat", "vert"),
            P("feat", None),
            P("feat"),
            P(None, "feat"),
        ),
        check_vma=False,
    )
```

profile of v0, /device:TPU:0, one launch (start us, length us, event | category | flops | bytes accessed | tf_op | source)
XLA Modules:
  0.0 159.4 jit_solution(17628341002482086971)
XLA Ops:
  7.2 0.0 copy-start
  7.2 0.7 compare_select_fusion.2
  7.9 0.1 reshape.139
  8.0 1.5 fusion.14
  9.5 0.5 copy.45
  10.0 0.9 gather_fusion
  10.9 0.1 copy.46
  11.0 0.7 reshape.173
  11.7 6.3 %all-to-all-start = ((bf16[4,2,1024]{2,1,0:T(2,128)(2,1)}), bf16[4,2,1024]{2,1,0:T(2,128)(2,1)S(1)}, u32[]{:S(2)}, u32[]{:S(2)}) async-start(bf16[4,2,1024]{2,1,0:T(2,128)(2,1)} %reshape.173), calls=%async_computation | async-start | bytes 32768 | tf_op jit(solution)/shard_map/all_to_all | solution.py:63
  18.7 4.9 %all-to-all-done = bf16[4,2,1024]{2,1,0:T(2,128)(2,1)S(1)} async-done(((bf16[4,2,1024]{2,1,0:T(2,128)(2,1)}), bf16[4,2,1024]{2,1,0:T(2,128)(2,1)S(1)}, u32[]{:S(2)}, u32[]{:S(2)}) %all-to-all-start) | async-done | bytes 16416 | tf_op jit(solution)/shard_map/all_to_all | solution.py:63
  23.6 0.1 reshape.174
  23.7 0.1 reshape.132
  23.9 1.0 gather_fusion.1
  24.9 0.0 copy-start.5
  24.9 7.9 %fusion.8 = bf16[32,256,128]{2,0,1:T(8,128)(2,1)S(1)} fusion(bf16[1,256,128,128]{3,2,1,0:T(8,128)(2,1)} %param.12, bf16[256,32,128]{2,1,0:T(8,128)(2,1)S(1)} %gather_fusion.1, pred[256]{0:T(512)(128)(4,1)S(1)} %compare_and_fusion.1), kind=kOutput, calls=%fused_computation.16 | convolution fusion | flops 269484032 | bytes 12583168 | tf_op jit(solution)/shard_map/dtc,trc->dtr/dot_general | solution.py:11
  32.8 0.7 fusion.22
  33.6 0.0 copy-start.3
  33.6 0.0 copy-start.7
  33.6 2.1 %convolution_convert_fusion = bf16[256,4096]{1,0:T(8,128)(2,1)} fusion(bf16[4,8,32,128]{3,2,1,0:T(8,128)(2,1)S(1)} %bitcast.79, bf16[256,256]{1,0:T(8,128)(2,1)S(1)} %copy-done, s32[]{:T(128)S(6)} %select_n.53), kind=kOutput, calls=%fused_computation.8 | convolution fusion | flops 68157440 | bytes 2375684 | tf_op jit(solution)/shard_map/dot_general | solution.py:71
  35.6 0.0 reduce-scatter.2.cloned.1.call-update
  35.7 0.0 all-gather.2.cloned.1.call-start
  35.7 39.6 %reduce-scatter.2.cloned.1.call-done = bf16[32,4096]{1,0:T(8,128)(2,1)} async-done(((bf16[256,4096]{1,0:T(8,128)(2,1)}), bf16[32,4096]{1,0:T(8,128)(2,1)}) %reduce-scatter.2.cloned.1.call-update) | async-done | bytes 262160 | tf_op jit(solution)/shard_map/reduce_scatter | solution.py:70
  75.4 2.2 %convert_reduce_fusion = (f32[32]{0:T(128)S(1)}, bf16[32,4096]{1,0:T(8,128)(2,1)}, bf16[32,4096]{1,0:T(8,128)(2,1)}) fusion(f32[32]{0:T(128)S(1)} %copy-done.7, bf16[32,4096]{1,0:T(8,128)(2,1)} %reduce-scatter.2.cloned.1.call-done, bf16[32,4096]{1,0:T(8,128)(2,1)S(1)} %copy-done.3), kind=kLoop, calls=%fused_computation.32 | loop fusion | flops 2097120 | bytes 1048832 | tf_op jit(solution)/shard_map/reduce_sum | solution.py:101
  77.5 0.0 all-gather.2.cloned.1.call-update
  77.6 28.3 %all-gather.2.cloned.1.call-done = bf16[256,4096]{1,0:T(8,128)(2,1)} async-done(((bf16[32,4096]{1,0:T(8,128)(2,1)}), bf16[256,4096]{1,0:T(8,128)(2,1)}) %all-gather.2.cloned.1.call-update) | async-done | bytes 2097168 | tf_op jit(solution)/shard_map/all_gather | solution.py:84
  105.9 2.1 %fusion.25 = bf16[4,32,8,128]{3,2,1,0:T(8,128)(2,1)S(1)} fusion(bf16[256,4096]{1,0:T(8,128)(2,1)} %all-gather.2.cloned.1.call-done, bf16[256,256]{1,0:T(8,128)(2,1)S(1)} %copy-done, s32[]{:T(128)S(6)} %select_n.53), kind=kOutput, calls=%fused_computation.28 | convolution fusion | flops 67239936 | bytes 2375684 | tf_op jit(solution)/shard_map/dot_general | solution.py:85
  108.0 1.0 gather_fusion.2
  109.0 5.7 %fusion.11 = bf16[32,256,128]{2,0,1:T(8,128)(2,1)S(1)} fusion(bf16[1,256,128,128]{3,2,1,0:T(8,128)(2,1)} %param.12, bf16[256,32,128]{2,1,0:T(8,128)(2,1)S(1)} %gather_fusion.2, pred[256]{0:T(512)(128)(4,1)S(1)} %compare_and_fusion), kind=kOutput, calls=%fused_computation.17 | convolution fusion | flops 269484032 | bytes 12583168 | tf_op jit(solution)/shard_map/dtr,trc->dtc/dot_general | solution.py:20
  114.8 0.7 fusion.4
  115.5 0.1 copy.82
  115.6 0.1 reshape.136
  115.7 0.7 reshape.175
  116.4 4.6 %all-to-all-start.1 = ((bf16[4,2,1024]{2,1,0:T(2,128)(2,1)}), bf16[4,2,1024]{2,1,0:T(2,128)(2,1)S(1)}, u32[]{:S(2)}, u32[]{:S(2)}) async-start(bf16[4,2,1024]{2,1,0:T(2,128)(2,1)} %reshape.175), calls=%async_computation.2 | async-start | bytes 32768 | tf_op jit(solution)/shard_map/all_to_all | solution.py:98
  121.0 0.7 fusion.28
  121.8 0.8 slice.15
  122.6 1.6 %copy.59 = f32[32,4096]{0,1:T(8,128)S(1)} copy(f32[32,4096]{1,0:T(8,128)} %slice.15) | data formatting | bytes 1048576
  124.2 0.0 copy-start.2
  124.3 0.0 copy-start.4
  124.3 2.4 %all-to-all-done.1 = bf16[4,2,1024]{2,1,0:T(2,128)(2,1)S(1)} async-done(((bf16[4,2,1024]{2,1,0:T(2,128)(2,1)}), bf16[4,2,1024]{2,1,0:T(2,128)(2,1)S(1)}, u32[]{:S(2)}, u32[]{:S(2)}) %all-to-all-start.1) | async-done | bytes 16416 | tf_op jit(solution)/shard_map/all_to_all | solution.py:98
  126.6 0.1 reshape.176
  126.8 0.1 copy.57
  126.9 2.7 %scatter_fusion = f32[32,4096]{0,1:T(8,128)S(1)} fusion(f32[32,4096]{0,1:T(8,128)S(1)} %copy.59, s32[256]{0:T(256)S(1)} %reshape.139, f32[256,32]{1,0:T(8,128)S(1)} %bitcast.83), kind=kCustom, calls=%fused_computation.3 | custom fusion | flops 8192 | bytes 99328 | tf_op jit(solution)/shard_map/scatter-add | solution.py:99
  129.6 1.4 copy.56
  130.9 2.3 %fusion.15 = (f32[4,32]{1,0:T(4,128)S(1)}, bf16[4,32,4096]{2,1,0:T(8,128)(2,1)}) fusion(bf16[4,32,4096]{2,1,0:T(8,128)(2,1)S(1)} %copy-done.2, f32[32,4096]{1,0:T(8,128)} %copy.56, f32[4,32]{1,0:T(4,128)S(1)} %copy-done.4), kind=kLoop, calls=%fused_computation.19 | loop fusion | flops 2621312 | bytes 2622464 | tf_op jit(solution)/shard_map/reduce_sum | solution.py:102
  133.3 17.6 %all-reduce = (f32[32,256]{1,0:T(8,128)S(1)}, f32[32]{0:T(128)S(1)}, f32[4,32]{1,0:T(4,128)S(1)}) all-reduce(f32[32,256]{1,0:T(8,128)S(1)} %fusion.28, f32[32]{0:T(128)S(1)} %get-tuple-element.8, f32[4,32]{1,0:T(4,128)S(1)} %get-tuple-element.10), channel_id=1, replica_groups=mesh['vert'=4,'feat'=8] {'vert'}, use_global_device_ids=true, to_apply=%region_3.4 | all-reduce | flops 8352 | bytes 66816 | tf_op jit(solution)/shard_map/psum | solution.py:103
  150.8 0.6 broadcast_multiply_fusion
  151.5 0.5 broadcast_multiply_fusion.2
  152.0 0.6 broadcast_multiply_fusion.1
  (26 shorter events, 0.2 us)
Async XLA Ops:
  7.2 26.4 %copy-start = (bf16[256,256]{1,0:T(8,128)(2,1)S(1)}, bf16[256,256]{1,0:T(8,128)(2,1)}, u32[]{:S(2)}) copy-start(bf16[256,256]{1,0:T(8,128)(2,1)} %param.17) | copy-start | bytes 393220
  7.2 11.5 %copy-start.6 = (s32[1,256]{1,0:T(1,128)S(1)}, s32[1,256]{1,0:T(1,128)}, u32[]{:S(2)}) copy-start(s32[1,256]{1,0:T(1,128)} %param.14) | copy-start | bytes 3076
  11.7 11.9 %all-to-all-start = ((bf16[4,2,1024]{2,1,0:T(2,128)(2,1)}), bf16[4,2,1024]{2,1,0:T(2,128)(2,1)S(1)}, u32[]{:S(2)}, u32[]{:S(2)}) async-start(bf16[4,2,1024]{2,1,0:T(2,128)(2,1)} %reshape.173), calls=%async_computation | async-start | bytes 32768 | tf_op jit(solution)/shard_map/all_to_all | solution.py:63
  18.0 57.4 %reduce-scatter.2.cloned.1.call-start = ((), (), s32[]{:S(2)}) async-start(), calls=%async_computation.3 | async-start | bytes 2359296 | tf_op jit(solution)/shard_map/reduce_scatter | solution.py:70
  24.9 7.9 %copy-start.5 = (s32[1,256]{1,0:T(1,128)S(1)}, s32[1,256]{1,0:T(1,128)}, u32[]{:S(2)}) copy-start(s32[1,256]{1,0:T(1,128)} %param.13) | copy-start | bytes 3076
  33.6 41.8 %copy-start.3 = (bf16[32,4096]{1,0:T(8,128)(2,1)S(1)}, bf16[32,4096]{1,0:T(8,128)(2,1)}, u32[]{:S(2)}) copy-start(bf16[32,4096]{1,0:T(8,128)(2,1)} %param.19) | copy-start | bytes 786436
  33.6 41.8 %copy-start.7 = (f32[32]{0:T(128)S(1)}, f32[32]{0:T(128)}, u32[]{:S(2)}) copy-start(f32[32]{0:T(128)} %param.18) | copy-start | bytes 388
  35.7 70.2 %all-gather.2.cloned.1.call-start = ((), (), s32[]{:S(2)}) async-start(), calls=%async_computation.4 | async-start | bytes 2359296 | tf_op jit(solution)/shard_map/all_gather | solution.py:84
  114.7 6.3 %copy-start.1 = (bf16[256,4096]{1,0:T(8,128)(2,1)S(1)}, bf16[256,4096]{1,0:T(8,128)(2,1)}, u32[]{:S(2)}) copy-start(bf16[256,4096]{1,0:T(8,128)(2,1)} %all-gather.2.cloned.1.call-done) | copy-start | bytes 6291460
  116.4 10.2 %all-to-all-start.1 = ((bf16[4,2,1024]{2,1,0:T(2,128)(2,1)}), bf16[4,2,1024]{2,1,0:T(2,128)(2,1)S(1)}, u32[]{:S(2)}, u32[]{:S(2)}) async-start(bf16[4,2,1024]{2,1,0:T(2,128)(2,1)} %reshape.175), calls=%async_computation.2 | async-start | bytes 32768 | tf_op jit(solution)/shard_map/all_to_all | solution.py:98
  124.2 6.7 %copy-start.2 = (bf16[4,32,4096]{2,1,0:T(8,128)(2,1)S(1)}, bf16[4,32,4096]{2,1,0:T(8,128)(2,1)}, u32[]{:S(2)}) copy-start(bf16[4,32,4096]{2,1,0:T(8,128)(2,1)} %param.10) | copy-start | bytes 3145732
  124.3 6.7 %copy-start.4 = (f32[4,32]{1,0:T(4,128)S(1)}, f32[4,32]{1,0:T(4,128)}, u32[]{:S(2)}) copy-start(f32[4,32]{1,0:T(4,128)} %param.11) | copy-start | bytes 1540
Sparse Core Ops, SparseCore 0:
  35.8 39.5 reduce-scatter.1
  78.0 27.8 all-gather.1
where the time goes:
time: 160 us; the launch traced here: 159 us
  waiting for transfers between devices  75.2 us (47%)
  matrix products  19.9 us (12%)
  blocking collectives  17.6 us (11%)
  between operations  15 us (9%)
  other arithmetic  11.3 us (7%)
  starting transfers between devices  11 us (7%)
  local copies, waits for them, and re-layouts  9.47 us (6%)
    reduce_scatter x1, waiting for transfers between devices, local(): lax.psum_scatter(lax.dot_general(weight_rows, aggregated, (((0,), (0,)),...  39.6 us
    all_gather x1, waiting for transfers between devices, local(): piece = lax.all_gather(grad_pre, 'feat', axis=0, tiled=True)  28.3 us
    psum x1, blocking collectives, local(): lax.psum((terms_now, bias_terms, depth_terms), 'vert')  17.6 us
    dot_general x1, matrix products, tile_forward(): jnp.einsum('dtc,trc->dtr', picked, tile_grp, preferred_element_type=jnp.f...  7.88 us
    all_to_all x1, starting transfers between devices, local(): lax.all_to_all(outgoing, 'vert', split_axis=1, concat_axis=1, tiled=True)  6.32 us
    dot_general x1, matrix products, tile_backward(): jnp.einsum('dtr,trc->dtc', picked, tile_grp, preferred_element_type=jnp.f...  5.73 us
    all_to_all x1, waiting for transfers between devices, local(): lax.all_to_all(outgoing, 'vert', split_axis=1, concat_axis=1, tiled=True)  4.89 us
    all_to_all x1, starting transfers between devices, local(): lax.all_to_all(halo_terms, 'vert', split_axis=1, concat_axis=1, tiled=True)  4.6 us
  transfers between devices with their start and end apart: 4, of which 4 were waited for; matrix products, arithmetic and copies ran while one was open for 2% of the time, Pallas kernels for 0%

commit v1 on v0

v1 whole, which is shorter than its diff:
```python
import functools
import math

import jax
import jax.numpy as jnp
from jax import lax
from jax.experimental import pallas as pl
from jax.experimental.pallas import tpu as pltpu
from jax.sharding import PartitionSpec as P

F32 = jnp.float32
BF16 = jnp.bfloat16
HALO_OUT, COT, BIAS, AGG, GRAD, LAYER, TERMS, HALO_BACK, SUMS, DEPTH = range(10)
TILE_PARTS = 8
UNROLL = 8


def whole_kernel(
    sizes,
    norm_scale,
    order_ref,
    block_ref,
    keep_ref,
    last_ref,
    has_ref,
    states_ref,
    depth_ref,
    rows_ref,
    rows_col_ref,
    weight_ref,
    bias_ref,
    cot_ref,
    tiles_hbm,
    layer_ref,
    grad_states_ref,
    grad_weight_ref,
    grad_bias_ref,
    grad_depth_ref,
    tiles,
    extended,
    running,
    halo_send,
    halo_recv,
    back_send,
    back_recv,
    cot_recv,
    bias_recv,
    agg_send,
    agg_recv,
    grad_send,
    grad_recv,
    layer_send,
    layer_recv,
    terms_send,
    terms_recv,
    sums_recv,
    depth_recv,
    grad_blocks,
    mixed_grad,
    weight_t,
    tile_sem,
    send_sem,
    recv_sem,
):
    vert, feat, channels, row_count, block, halo = sizes
    state_count = states_ref.shape[0]
    capacity = tiles.shape[0]
    width = row_count // feat
    features = channels * feat
    row_blocks = row_count // block
    src_blocks = extended.shape[0]
    slots = vert * halo
    per_block = block // halo
    per_width = width // block
    my_vert = lax.axis_index("vert")
    my_feat = lax.axis_index("feat")

    def vert_peer(k):
        return lax.rem(my_vert + k, vert)

    def feat_peer(k):
        return lax.rem(my_feat + k, feat)

    def vert_copy(kind, k, src, dst):
        return pltpu.make_async_remote_copy(
            src_ref=src,
            dst_ref=dst,
            send_sem=send_sem.at[kind, k],
            recv_sem=recv_sem.at[kind, k],
            device_id=(vert_peer(k), my_feat),
            device_id_type=pl.DeviceIdType.MESH,
        )

    def feat_copy(kind, k, src, dst):
        return pltpu.make_async_remote_copy(
            src_ref=src,
            dst_ref=dst,
            send_sem=send_sem.at[kind, k],
            recv_sem=recv_sem.at[kind, k],
            device_id=(my_vert, feat_peer(k)),
            device_id_type=pl.DeviceIdType.MESH,
        )

    def vert_exchange(kind, send, recv):
        copies = [
            vert_copy(kind, k, send.at[vert_peer(k)], recv.at[my_vert]) for k in range(1, vert)
        ]
        for copy in copies:
            copy.start()
        return copies

    def vert_spread(kind, recv):
        copies = [
            vert_copy(kind, k, recv.at[my_vert], recv.at[my_vert]) for k in range(1, vert)
        ]
        for copy in copies:
            copy.start()
        return copies

    def feat_exchange(kind, send, recv):
        copies = [
            feat_copy(kind, k, send.at[feat_peer(k)], recv.at[my_feat]) for k in range(1, feat)
        ]
        for copy in copies:
            copy.start()
        return copies

    def arrived(copies):
        for copy in copies:
            copy.wait_recv()

    barrier = pltpu.get_barrier_semaphore()
    for k in range(1, vert):
        pl.semaphore_signal(
            barrier, inc=1, device_id=(vert_peer(k), my_feat), device_id_type=pl.DeviceIdType.MESH
        )
    for k in range(1, feat):
        pl.semaphore_signal(
            barrier, inc=1, device_id=(my_vert, feat_peer(k)), device_id_type=pl.DeviceIdType.MESH
        )

    part = capacity // TILE_PARTS
    tile_copies = [
        pltpu.make_async_copy(
            tiles_hbm.at[0, pl.ds(i * part, part)], tiles.at[pl.ds(i * part, part)], tile_sem.at[i]
        )
        for i in range(TILE_PARTS)
    ]
    for copy in tile_copies:
        copy.start()

    depth = [depth_ref[:, j : j + 1] for j in range(state_count)]
    rows = rows_ref[...]
    step = 2 * block

    def mix(i, picked):
        start = pl.multiple_of(i * step, step)
        total = depth[0] * states_ref[0, :, pl.ds(start, step)].astype(F32)
        for j in range(1, state_count):
            total += depth[j] * states_ref[j, :, pl.ds(start, step)].astype(F32)
        mixed = total.astype(BF16)
        extended[2 * i] = mixed[:, :block]
        extended[2 * i + 1] = mixed[:, block:]
        here = lax.broadcasted_iota(jnp.int32, (step, slots), 0) + start
        onehot = jnp.where(here == rows, 1.0, 0.0).astype(BF16)
        return picked + jnp.dot(mixed, onehot, preferred_element_type=F32)

    picked = lax.fori_loop(
        0, row_count // step, mix, jnp.zeros((channels, slots), F32), unroll=2
    ).astype(BF16)
    for p in range(vert):
        halo_send[p] = picked[:, p * halo : (p + 1) * halo]

    pl.semaphore_wait(barrier, vert + feat - 2)
    halo_copies = vert_exchange(HALO_OUT, halo_send, halo_recv)
    cot_copies = [
        feat_copy(
            COT,
            k,
            cot_ref.at[:, pl.ds(pl.multiple_of(feat_peer(k) * width, width), width)],
            cot_recv.at[my_feat],
        )
        for k in range(1, feat)
    ]
    bias_recv[my_feat] = bias_ref[...]
    bias_copies = [
        feat_copy(BIAS, k, bias_recv.at[my_feat], bias_recv.at[my_feat]) for k in range(1, feat)
    ]
    for copy in cot_copies + bias_copies:
        copy.start()
    halo_recv[my_vert] = halo_send[my_vert]
    cot_recv[my_feat] = cot_ref[:, pl.ds(pl.multiple_of(my_feat * width, width), width)]
    weight = weight_ref[...]
    weight_t[...] = weight.astype(F32).T.astype(BF16)

    arrived(halo_copies)
    for j in range(src_blocks - row_blocks):
        extended[row_blocks + j] = jnp.concatenate(
            [halo_recv[j * per_block + h] for h in range(per_block)], axis=1
        )
    for copy in tile_copies:
        copy.wait()

    def tile_pass(base, source, dims):
        def group(g, total):
            for u in range(UNROLL):
                k = g * UNROLL + u
                product = lax.dot_general(
                    source[block_ref[base + k]],
                    tiles[order_ref[base + k]],
                    (dims, ((), ())),
                    preferred_element_type=F32,
                )
                total = total * keep_ref[base + k] + product
                running[k] = total
            return total

        lax.fori_loop(0, capacity // UNROLL, group, jnp.zeros((channels, block), F32))

    tile_pass(0, extended, ((1,), (1,)))
    for n in range(row_blocks):
        j = n % per_width
        agg_send[n // per_width, :, j * block : (j + 1) * block] = (
            running[last_ref[n]] * has_ref[n]
        ).astype(BF16)
    agg_copies = feat_exchange(AGG, agg_send, agg_recv)
    agg_recv[my_feat] = agg_send[my_feat]
    arrived(cot_copies)
    arrived(bias_copies)
    arrived(agg_copies)

    aggregated = agg_recv[...].reshape(features, width)
    bias = bias_recv[...].reshape(features, block)[:, :1]
    pre_act = jnp.dot(weight_t[...], aggregated, preferred_element_type=F32) + bias
    sigmoid_pre = jax.nn.sigmoid(pre_act)
    grad_pre32 = (
        cot_recv[...].reshape(features, width).astype(F32)
        * sigmoid_pre
        * (1.0 + pre_act * (1.0 - sigmoid_pre))
    )
    grad_pre = grad_pre32.astype(BF16)
    grad_send[...] = (
        jnp.dot(weight, grad_pre, preferred_element_type=F32)
        .astype(BF16)
        .reshape(feat, channels, width)
    )
    grad_copies = feat_exchange(GRAD, grad_send, grad_recv)
    grad_recv[my_feat] = grad_send[my_feat]
    layer_send[...] = (pre_act * sigmoid_pre).astype(BF16).reshape(feat, channels, width)
    layer_copies = feat_exchange(LAYER, layer_send, layer_recv)
    layer_recv[my_feat] = layer_send[my_feat]
    terms_send[:, :, :features] = lax.dot_general(
        aggregated, grad_pre, (((1,), (1,)), ((), ())), preferred_element_type=F32
    ).reshape(feat, channels, features)
    terms_send[:, :, features:] = jnp.broadcast_to(
        jnp.sum(grad_pre.astype(F32), axis=1, keepdims=True), (features, block)
    ).reshape(feat, channels, block)
    terms_copies = feat_exchange(TERMS, terms_send, terms_recv)
    terms_recv[my_feat] = terms_send[my_feat]

    arrived(grad_copies)
    for n in range(row_blocks):
        j = n % per_width
        grad_blocks[n] = grad_recv[n // per_width, :, j * block : (j + 1) * block]
    tile_pass(capacity, grad_blocks, ((1,), (0,)))

    for s in range(row_blocks, src_blocks):
        value = (running[last_ref[src_blocks + s]] * has_ref[src_blocks + s]).astype(BF16)
        for h in range(per_block):
            back_send[(s - row_blocks) * per_block + h] = value[:, h * halo : (h + 1) * halo]
    back_copies = vert_exchange(HALO_BACK, back_send, back_recv)
    back_recv[my_vert] = back_send[my_vert]
    for s in range(row_blocks):
        mixed_grad[:, s * block : (s + 1) * block] = (
            running[last_ref[src_blocks + s]] * has_ref[src_blocks + s]
        )

    arrived(terms_copies)
    total = terms_recv[0]
    for f in range(1, feat):
        total += terms_recv[f]
    sums_recv[my_vert] = total
    sums_copies = vert_spread(SUMS, sums_recv)
    arrived(layer_copies)
    for f in range(feat):
        layer_ref[:, f * width : (f + 1) * width] = layer_recv[f]

    arrived(back_copies)
    returned = jnp.concatenate([back_recv[q] for q in range(vert)], axis=1)
    rows_col = rows_col_ref[...]

    def finish(i, sums):
        start = pl.multiple_of(i * step, step)
        here = lax.broadcasted_iota(jnp.int32, (slots, step), 1) + start
        onehot = jnp.where(here == rows_col, 1.0, 0.0).astype(BF16)
        grad_mixed = mixed_grad[:, pl.ds(start, step)] + jnp.dot(
            returned, onehot, preferred_element_type=F32
        )
        out = []
        for j in range(state_count):
            grad_states_ref[j, :, pl.ds(start, step)] = (depth[j] * grad_mixed).astype(BF16)
            term = states_ref[j, :, pl.ds(start, step)].astype(F32) * grad_mixed
            term = term[:, :block] + term[:, block:]
            out.append(sums[j] + term)
        return tuple(out)

    sums = lax.fori_loop(
        0,
        row_count // step,
        finish,
        tuple(jnp.zeros((channels, block), F32) for _ in range(state_count)),
        unroll=2,
    )
    lane = lax.broadcasted_iota(jnp.int32, (channels, block), 1)
    packed = jnp.zeros((channels, block), F32)
    for j in range(state_count):
        packed = jnp.where(lane == j, jnp.sum(sums[j], axis=1, keepdims=True), packed)
    depth_recv[my_vert] = packed
    depth_copies = vert_spread(DEPTH, depth_recv)

    arrived(sums_copies)
    total = sums_recv[0]
    for q in range(1, vert):
        total += sums_recv[q]
    grad_weight_ref[...] = total[:, :features] * norm_scale
    grad_bias_ref[...] = total[:, features:] * norm_scale
    arrived(depth_copies)
    total = depth_recv[0]
    for q in range(1, vert):
        total += depth_recv[q]
    grad_depth_ref[...] = total * norm_scale
    for copies in (
        halo_copies,
        cot_copies,
        bias_copies,
        agg_copies,
        grad_copies,
        layer_copies,
        terms_copies,
        back_copies,
        sums_copies,
        depth_copies,
    ):
        for copy in copies:
            copy.wait_send()


def sort_tiles(keys, others, key_count):
    capacity = keys.shape[1]
    spot = jnp.arange(capacity, dtype=jnp.int32)
    full = keys * capacity + spot[None, :]
    rank = jnp.sum((full[:, None, :] < full[:, :, None]).astype(jnp.int32), axis=2)
    packed = (spot[None, :] * 128 + keys) * 128 + others
    chosen = rank[:, None, :] == spot[None, :, None]
    packed = jnp.sum(jnp.where(chosen, packed[:, None, :], 0), axis=2)
    order = packed // (128 * 128)
    sorted_keys = (packed // 128) % 128
    other = packed % 128
    before = jnp.concatenate([jnp.full((2, 1), -1, jnp.int32), sorted_keys[:, :-1]], axis=1)
    keep = (sorted_keys == before).astype(F32)
    bins = jnp.arange(key_count, dtype=jnp.int32)[None, :, None]
    upto = jnp.sum((keys[:, None, :] <= bins).astype(jnp.int32), axis=2)
    has = jnp.any(keys[:, None, :] == bins, axis=2).astype(F32)
    last = jnp.maximum(upto - 1, 0)
    return [a.reshape(-1) for a in (order, other, keep, last, has)]


def local(
    states,
    depth_weight,
    tile_values,
    tile_dst,
    tile_src,
    tile_count,
    send_rows,
    weight,
    bias_vec,
    cotangent,
):
    state_count, channels, row_count = states.shape
    capacity, block = tile_values.shape[1], tile_values.shape[2]
    vert, feat = lax.axis_size("vert"), lax.axis_size("feat")
    halo = send_rows.shape[2]
    slots = send_rows.shape[1] * halo
    width = row_count // feat
    features = channels * feat
    row_blocks = row_count // block
    src_blocks = (row_count + slots) // block
    norm_scale = 1.0 / math.sqrt(vert * row_count)

    live = jnp.arange(capacity, dtype=jnp.int32)[None, :] < tile_count[0]
    both = jnp.concatenate([tile_dst, tile_src], axis=0)
    keys = jnp.where(live, both, src_blocks)
    others = jnp.concatenate([tile_src, tile_dst], axis=0)
    scalars = sort_tiles(keys, others, src_blocks)

    vmem = pl.BlockSpec(memory_space=pltpu.VMEM)
    smem = pl.BlockSpec(memory_space=pltpu.SMEM)
    most = max(vert, feat)
    terms = features + block
    layer, grad_states, grad_weight, grad_bias, grad_depth = pl.pallas_call(
        functools.partial(
            whole_kernel, (vert, feat, channels, row_count, block, halo), norm_scale
        ),
        out_shape=(
            jax.ShapeDtypeStruct((channels, row_count), BF16),
            jax.ShapeDtypeStruct((state_count, channels, row_count), BF16),
            jax.ShapeDtypeStruct((channels, features), F32),
            jax.ShapeDtypeStruct((channels, block), F32),
            jax.ShapeDtypeStruct((channels, block), F32),
        ),
        in_specs=[smem] * 5 + [vmem] * 7 + [pl.BlockSpec(memory_space=pl.ANY)],
        out_specs=(vmem,) * 5,
        scratch_shapes=[
            pltpu.VMEM((capacity, block, block), BF16),
            pltpu.VMEM((src_blocks, channels, block), BF16),
            pltpu.VMEM((capacity, channels, block), F32),
            pltpu.VMEM((vert, channels, halo), BF16),
            pltpu.VMEM((vert, channels, halo), BF16),
            pltpu.VMEM((vert, channels, halo), BF16),
            pltpu.VMEM((vert, channels, halo), BF16),
            pltpu.VMEM((feat, channels, width), BF16),
            pltpu.VMEM((feat, channels, block), F32),
            pltpu.VMEM((feat, channels, width), BF16),
            pltpu.VMEM((feat, channels, width), BF16),
            pltpu.VMEM((feat, channels, width), BF16),
            pltpu.VMEM((feat, channels, width), BF16),
            pltpu.VMEM((feat, channels, width), BF16),
            pltpu.VMEM((feat, channels, width), BF16),
            pltpu.VMEM((feat, channels, terms), F32),
            pltpu.VMEM((feat, channels, terms), F32),
            pltpu.VMEM((vert, channels, terms), F32),
            pltpu.VMEM((vert, channels, block), F32),
            pltpu.VMEM((row_blocks, channels, block), BF16),
            pltpu.VMEM((channels, row_count), F32),
            pltpu.VMEM((features, features), BF16),
            pltpu.SemaphoreType.DMA((TILE_PARTS,)),
            pltpu.SemaphoreType.DMA((10, most)),
            pltpu.SemaphoreType.DMA((10, most)),
        ],
        compiler_params=pltpu.CompilerParams(
            collective_id=0, has_side_effects=True, vmem_limit_bytes=48 * 1024 * 1024
        ),
    )(
        *scalars,
        states,
        depth_weight.T,
        send_rows.reshape(1, slots),
        send_rows.reshape(slots, 1),
        weight,
        jnp.broadcast_to(bias_vec[:, None], (channels, block)),
        cotangent,
        tile_values,
    )
    return layer, grad_states, grad_weight, grad_bias[:, 0], grad_depth[:, :state_count].T


def solution(mesh):
    placed = (
        P(None, "feat", "vert"),
        P(None, "feat"),
        P("vert", None, None, None),
        P("vert", None),
        P("vert", None),
        P("vert"),
        P("vert", None, None),
        P(),
        P("feat"),
        P("feat", "vert"),
    )
    return jax.shard_map(
        local,
        mesh=mesh,
        in_specs=placed,
        out_specs=(
            P("feat", "vert"),
            P(None, "feat", "vert"),
            P("feat", None),
            P("feat"),
            P(None, "feat"),
        ),
        check_vma=False,
    )
```

time: 160 us -> 58.2 us (0.36)
  waiting for transfers between devices: 75.2 us -> 0 us
  Pallas kernels: 0 us -> 45.1 us
  matrix products: 19.9 us -> 0 us
  blocking collectives: 17.6 us -> 0 us
  between operations: 15 us -> 1.34 us
  starting transfers between devices: 11 us -> 0 us
  other arithmetic: 11.3 us -> 1.53 us
    pallas_call x0 -> x1, Pallas kernels: none -> 45.1 us  [local(): pl.pallas_call(functools.partial(whole_kernel, (vert, feat, channels, row...]
    reduce_scatter x1 -> x0, waiting for transfers between devices: 39.6 us -> none  [local(): lax.psum_scatter(lax.dot_general(weight_rows, aggregated, (((0,), (0,)),...]
    all_gather x1 -> x0, waiting for transfers between devices: 28.3 us -> none  [local(): piece = lax.all_gather(grad_pre, 'feat', axis=0, tiled=True)]
    dot_general x7 -> x0, matrix products: 19.9 us -> none  [the longest x1 7.88 us: tile_forward(): jnp.einsum('dtc,trc->dtr', picked, tile_grp, preferred_element_type=jnp.f...]
    psum x1 -> x0, blocking collectives: 17.6 us -> none  [local(): lax.psum((terms_now, bias_terms, depth_terms), 'vert')]
    all_to_all x2 -> x0, starting transfers between devices: 10.9 us -> none  [the longest x1 6.32 us: local(): lax.all_to_all(outgoing, 'vert', split_axis=1, concat_axis=1, tiled=True)]
    all_to_all x2 -> x0, waiting for transfers between devices: 7.26 us -> none  [the longest x1 4.89 us: local(): lax.all_to_all(outgoing, 'vert', split_axis=1, concat_axis=1, tiled=True)]
    reduce_sum x3, other arithmetic: 6.05 us -> 0.52 us  [the longest x1 0.25 us: sort_tiles(): jnp.sum((full[:, None, :] < full[:, :, None]).astype(jnp.int32), axis=2)]
  transfers between devices with their start and end apart: 4 -> 0, of which waited for: 4 -> 0; matrix products, arithmetic and copies ran while one was open for 2% -> 0% of each run, Pallas kernels for 0% -> 0%
where the time goes in v1:
time: 58.2 us; the launch traced here: 57.9 us
  Pallas kernels  45.1 us (77%)
  local copies, waits for them, and re-layouts  9.88 us (17%)
  other arithmetic  1.53 us (3%)
  between operations  1.34 us (2%)
    pallas_call x1, Pallas kernels, local(): pl.pallas_call(functools.partial(whole_kernel, (vert, feat, channels, row...  45.1 us
    unnamed x13, local copies, waits for them, and re-layouts  6.78 us

profile of v1, /device:TPU:0, one launch (start us, length us, event | category | flops | bytes accessed | tf_op | source)
XLA Modules:
  0.0 57.9 jit_solution(15252524123578736023)
XLA Ops:
  1.3 0.8 %reshape.182.rows_ref = s32[1,256]{1,0:T(1,128)S(1)} reshape(s32[1,4,64]{2,1,0:T(4,128)} %param.16) | data formatting | bytes 2048 | tf_op jit(solution)/shard_map/reshape | solution.py:448
  2.1 0.8 %add_select_fusion.2 = (s32[2,256]{1,0:T(2,128)S(1)}, s32[2,256]{1,0:T(2,128)S(1)}, s32[2,256]{1,0:T(2,128)S(1)}) fusion(s32[1,256]{1,0:T(1,128)} %param.14, s32[1,256]{1,0:T(1,128)} %param.13, pred[256]{0:T(512)(128)(4,1)S(1)} %iota_compare_fusion.3, s32[256]{0:T(256)S(1)} %iota_multiply_fusion), kind=kLoop, calls=%fused_computation.26 | loop fusion | flops 4096 | bytes 9472 | tf_op jit(solution)/shard_map/jit(_where)/select_n | solution.py:393
  2.8 0.2 convert_reduce_fusion
  3.1 0.2 select_reduce_fusion
  3.2 0.1 fusion
  3.4 0.1 convert_reduce_fusion.1
  3.5 0.1 max.12.last_ref
  3.6 0.1 reshape.186.has_ref
  3.7 0.1 fusion.2
  3.8 0.8 %copy.27 = f32[4,32]{0,1:T(8,128)S(1)} copy(f32[4,32]{1,0:T(4,128)} %param.11) | data formatting | bytes 1024 | tf_op args[1]
  4.5 0.7 %broadcast_in_dim.30.bias_ref = f32[32,128]{1,0:T(8,128)S(1)} broadcast(f32[32]{0:T(128)} %param.18), dimensions={0} | broadcast | bytes 16512 | tf_op jit(solution)/shard_map/broadcast_in_dim | solution.py:451
  5.3 0.8 %reshape.187.rows_col_ref = s32[256,1]{1,0:T(8,128)S(1)} reshape(s32[1,4,64]{2,1,0:T(4,128)} %param.16) | data formatting | bytes 2048 | tf_op jit(solution)/shard_map/reshape | solution.py:449
  6.1 0.0 copy-start
  6.1 1.2 %copy-done = bf16[4,32,4096]{2,1,0:T(8,128)(2,1)S(1)} copy-done((bf16[4,32,4096]{2,1,0:T(8,128)(2,1)S(1)}, bf16[4,32,4096]{2,1,0:T(8,128)(2,1)}, u32[]{:S(2)}) %copy-start) | copy-done | bytes 1048600
  7.3 0.0 copy-start.1
  7.3 0.9 %copy-done.1 = bf16[32,4096]{1,0:T(8,128)(2,1)S(1)} copy-done((bf16[32,4096]{1,0:T(8,128)(2,1)S(1)}, bf16[32,4096]{1,0:T(8,128)(2,1)}, u32[]{:S(2)}) %copy-start.1) | copy-done | bytes 262168
  8.3 0.0 copy-start.2
  8.3 0.9 %copy-done.2 = bf16[256,256]{1,0:T(8,128)(2,1)S(1)} copy-done((bf16[256,256]{1,0:T(8,128)(2,1)S(1)}, bf16[256,256]{1,0:T(8,128)(2,1)}, u32[]{:S(2)}) %copy-start.2) | copy-done | bytes 131096
  9.2 45.1 %shard_map.137 = (bf16[32,4096]{1,0:T(8,128)(2,1)S(1)}, bf16[4,32,4096]{2,1,0:T(8,128)(2,1)S(1)}, f32[32,256]{1,0:T(8,128)S(1)}, f32[32,128]{1,0:T(8,128)S(1)}, f32[32,128]{1,0:T(8,128)S(1)}) custom-call(s32[512]{0:T(512)S(1)} %get-tuple-element.39.order_ref, s32[512]{0:T(512)S(1)} %get-tuple-element.38.block_ref, f32[512]{0:T(512)S(1)} %bitcast.12, ...), custom_call_target="tpu_custom_call" | custom-call | tf_op jit(solution)/shard_map/pallas_call | solution.py:401
  54.3 0.6 %slice_reduce_fusion = f32[32]{0:T(128)} fusion(f32[32,128]{1,0:T(8,128)S(1)} %get-tuple-element.13), kind=kLoop, calls=%fused_computation.8 | loop fusion | bytes 256 | tf_op jit(solution)/shard_map/slice | solution.py:455
  54.9 0.7 %copy.29 = f32[4,32]{1,0:T(4,128)} copy(f32[4,32]{0,1:T(8,128)S(1)} %slice_bitcast_fusion) | data formatting | bytes 1024
  55.6 0.7 %copy.37 = bf16[32,4096]{1,0:T(8,128)(2,1)} copy(bf16[32,4096]{1,0:T(8,128)(2,1)S(1)} %get-tuple-element.45) | data formatting | bytes 524288
  56.3 1.0 %copy.38 = bf16[4,32,4096]{2,1,0:T(8,128)(2,1)} copy(bf16[4,32,4096]{2,1,0:T(8,128)(2,1)S(1)} %get-tuple-element.46) | data formatting | bytes 2097152
  57.2 0.6 %copy.39 = f32[32,256]{1,0:T(8,128)} copy(f32[32,256]{1,0:T(8,128)S(1)} %get-tuple-element.47) | data formatting | bytes 65536
  (9 shorter events, 0.1 us)
Async XLA Ops:
  6.1 1.2 %copy-start = (bf16[4,32,4096]{2,1,0:T(8,128)(2,1)S(1)}, bf16[4,32,4096]{2,1,0:T(8,128)(2,1)}, u32[]{:S(2)}) copy-start(bf16[4,32,4096]{2,1,0:T(8,128)(2,1)} %states_ref.1) | copy-start | bytes 3145732
  7.3 0.9 %copy-start.1 = (bf16[32,4096]{1,0:T(8,128)(2,1)S(1)}, bf16[32,4096]{1,0:T(8,128)(2,1)}, u32[]{:S(2)}) copy-start(bf16[32,4096]{1,0:T(8,128)(2,1)} %cot_ref.1) | copy-start | bytes 786436
  8.3 0.9 %copy-start.2 = (bf16[256,256]{1,0:T(8,128)(2,1)S(1)}, bf16[256,256]{1,0:T(8,128)(2,1)}, u32[]{:S(2)}) copy-start(bf16[256,256]{1,0:T(8,128)(2,1)} %weight_ref.1) | copy-start | bytes 393220

commit v2 on v1

--- a/solution.py
+++ b/solution.py
@@ -12,27 +12,81 @@
 BF16 = jnp.bfloat16
 HALO_OUT, COT, BIAS, AGG, GRAD, LAYER, TERMS, HALO_BACK, SUMS, DEPTH = range(10)
 TILE_PARTS = 8
-UNROLL = 8
+GROUPS = 6
+VMEM_LIMIT = 63 * 1024 * 1024
+STRIDE = 128
+MIX_UNROLL = 8
+
+
+def diagonal(size):
+    down = lax.broadcasted_iota(jnp.int32, (size, size), 0)
+    return down == lax.broadcasted_iota(jnp.int32, (size, size), 1)
+
+
+def column_of(row):
+    size = row.shape[1]
+    spread = jnp.broadcast_to(row, (size, size))
+    return jnp.sum(jnp.where(diagonal(size), spread, 0.0), axis=1, keepdims=True)
+
+
+def row_of(column):
+    size = column.shape[0]
+    spread = jnp.broadcast_to(column, (size, size))
+    return jnp.sum(jnp.where(diagonal(size), spread, 0.0), axis=0, keepdims=True)
+
+
+def plan_tiles(tile_total, dst, src, plan_vec):
+    capacity = dst.shape[1]
+    lanes = plan_vec.shape[1]
+    live = lax.broadcasted_iota(jnp.int32, (1, capacity), 1) < tile_total
+    dead = float(STRIDE - 1)
+    dst, src = dst.astype(F32), src.astype(F32)
+    dst_key, src_key = jnp.where(live, dst, dead), jnp.where(live, src, dead)
+    down = lax.broadcasted_iota(jnp.int32, (STRIDE, capacity), 0)
+    stacked = jnp.where(down == 0, dst_key, jnp.where(down == 1, src_key, 0.0))
+    stacked = jnp.where(down == 2, dst, jnp.where(down == 3, src, stacked))
+    turned = stacked.T
+    square = (capacity, capacity)
+    earlier = lax.broadcasted_iota(jnp.int32, square, 1) < lax.broadcasted_iota(
+        jnp.int32, square, 0
+    )
+    place = lax.broadcasted_iota(jnp.int32, (capacity, 1), 0).astype(F32)
+    bins = lax.broadcasted_iota(jnp.int32, (capacity, STRIDE), 1).astype(F32)
+    spots = lax.broadcasted_iota(jnp.int32, (capacity, lanes), 1).astype(F32)
+    plan_vec[...] = jnp.zeros(plan_vec.shape, jnp.int32)
+    for row, key_row, key, other in (
+        (0, dst_key, turned[:, 0:1], turned[:, 3:4]),
+        (2, src_key, turned[:, 1:2], turned[:, 2:3]),
+    ):
+        same = jnp.where((key_row == key) & earlier, 1.0, 0.0)
+        inside = jnp.sum(same, axis=1, keepdims=True)
+        counts = jnp.sum(jnp.where(bins == key, 1.0, 0.0), axis=0, keepdims=True)
+        pairs = jnp.floor((counts + 1.0) * 0.5)
+        first = jnp.sum(jnp.where(bins < key, pairs, 0.0), axis=1, keepdims=True)
+        spot = jnp.where(key == dead, -1.0, 2.0 * first + inside)
+        word = (2.0 * place + jnp.where(inside > 0.0, 1.0, 0.0)) * STRIDE + other + 1.0
+        words = jnp.sum(jnp.where(spots == spot, word, 0.0), axis=0, keepdims=True)
+        plan_vec[row : row + 1, :] = words.astype(jnp.int32)
+        after = jnp.floor(spot * 0.5) + 1.0
+        last = jnp.max(jnp.where(bins == key, after, 0.0), axis=0, keepdims=True)
+        plan_vec[row + 1 : row + 2, :STRIDE] = last.astype(jnp.int32)
 
 
 def whole_kernel(
     sizes,
     norm_scale,
-    order_ref,
-    block_ref,
-    keep_ref,
-    last_ref,
-    has_ref,
-    states_ref,
+    count_ref,
+    dst_ref,
+    src_ref,
     depth_ref,
     rows_ref,
-    rows_col_ref,
-    weight_ref,
+    weight_hbm,
     bias_ref,
-    cot_ref,
+    states_hbm,
+    cot_hbm,
     tiles_hbm,
     layer_ref,
-    grad_states_ref,
+    mixed_grad,
     grad_weight_ref,
     grad_bias_ref,
     grad_depth_ref,
@@ -56,9 +110,13 @@
     sums_recv,
     depth_recv,
     grad_blocks,
-    mixed_grad,
     weight_t,
+    weight_ref,
+    states_ref,
+    plan_vec,
+    plan,
     tile_sem,
+    local_sem,
     send_sem,
     recv_sem,
 ):
@@ -68,7 +126,8 @@
     width = row_count // feat
     features = channels * feat
     row_blocks = row_count // block
-    src_blocks = extended.shape[0]
+    src_blocks = extended.shape[0] - 1
+    unroll = (running.shape[0] - 1) // GROUPS
     slots = vert * halo
     per_block = block // halo
     per_width = width // block
@@ -139,6 +198,23 @@
             barrier, inc=1, device_id=(my_vert, feat_peer(k)), device_id_type=pl.DeviceIdType.MESH
         )
 
+    half = row_count // 2
+    states_copies = [
+        pltpu.make_async_copy(
+            states_hbm.at[:, :, pl.ds(i * half, half)],
+            states_ref.at[:, :, pl.ds(i * half, half)],
+            local_sem.at[i],
+        )
+        for i in range(2)
+    ]
+    weight_copy = pltpu.make_async_copy(weight_hbm, weight_ref, local_sem.at[2])
+    own_cot = pltpu.make_async_copy(
+        cot_hbm.at[:, pl.ds(pl.multiple_of(my_feat * width, width), width)],
+        cot_recv.at[my_feat],
+        local_sem.at[3],
+    )
+    for copy in states_copies + [weight_copy, own_cot]:
+        copy.start()
     part = capacity // TILE_PARTS
     tile_copies = [
         pltpu.make_async_copy(
@@ -149,8 +225,10 @@
     for copy in tile_copies:
         copy.start()
 
-    depth = [depth_ref[:, j : j + 1] for j in range(state_count)]
-    rows = rows_ref[...]
+    depth = [column_of(depth_ref[j : j + 1, :]) for j in range(state_count)]
+    rows = jnp.concatenate([rows_ref[0, p : p + 1, :] for p in range(vert)], axis=1)
+    extended[0] = jnp.zeros((channels, block), BF16)
+    running[0] = jnp.zeros((channels, block), F32)
     step = 2 * block
 
     def mix(i, picked):
@@ -159,15 +237,19 @@
         for j in range(1, state_count):
             total += depth[j] * states_ref[j, :, pl.ds(start, step)].astype(F32)
         mixed = total.astype(BF16)
-        extended[2 * i] = mixed[:, :block]
-        extended[2 * i + 1] = mixed[:, block:]
+        extended[2 * i + 1] = mixed[:, :block]
+        extended[2 * i + 2] = mixed[:, block:]
         here = lax.broadcasted_iota(jnp.int32, (step, slots), 0) + start
         onehot = jnp.where(here == rows, 1.0, 0.0).astype(BF16)
         return picked + jnp.dot(mixed, onehot, preferred_element_type=F32)
 
+    steps = row_count // step
+    states_copies[0].wait()
     picked = lax.fori_loop(
-        0, row_count // step, mix, jnp.zeros((channels, slots), F32), unroll=2
-    ).astype(BF16)
+        0, steps // 2, mix, jnp.zeros((channels, slots), F32), unroll=MIX_UNROLL
+    )
+    states_copies[1].wait()
+    picked = lax.fori_loop(steps // 2, steps, mix, picked, unroll=MIX_UNROLL).astype(BF16)
     for p in range(vert):
         halo_send[p] = picked[:, p * halo : (p + 1) * halo]
 
@@ -177,52 +259,68 @@
         feat_copy(
             COT,
             k,
-            cot_ref.at[:, pl.ds(pl.multiple_of(feat_peer(k) * width, width), width)],
+            cot_hbm.at[:, pl.ds(pl.multiple_of(feat_peer(k) * width, width), width)],
             cot_recv.at[my_feat],
         )
         for k in range(1, feat)
     ]
-    bias_recv[my_feat] = bias_ref[...]
+    bias_recv[my_feat] = jnp.broadcast_to(column_of(bias_ref[...]), (channels, block))
     bias_copies = [
         feat_copy(BIAS, k, bias_recv.at[my_feat], bias_recv.at[my_feat]) for k in range(1, feat)
     ]
     for copy in cot_copies + bias_copies:
         copy.start()
     halo_recv[my_vert] = halo_send[my_vert]
-    cot_recv[my_feat] = cot_ref[:, pl.ds(pl.multiple_of(my_feat * width, width), width)]
+    plan_tiles(count_ref[0], dst_ref[...], src_ref[...], plan_vec)
+    plan_copy = pltpu.make_async_copy(plan_vec, plan, local_sem.at[4])
+    plan_copy.start()
+    weight_copy.wait()
+    own_cot.wait()
     weight = weight_ref[...]
     weight_t[...] = weight.astype(F32).T.astype(BF16)
 
     arrived(halo_copies)
     for j in range(src_blocks - row_blocks):
-        extended[row_blocks + j] = jnp.concatenate(
+        extended[row_blocks + j + 1] = jnp.concatenate(
             [halo_recv[j * per_block + h] for h in range(per_block)], axis=1
         )
     for copy in tile_copies:
         copy.wait()
 
-    def tile_pass(base, source, dims):
+    plan_copy.wait()
+
+    def closing(row, n):
+        return running[jnp.clip(plan[row, n], 0, running.shape[0] - 1)]
+
+    def tile_pass(row, source, dims):
+        def pick(k):
+            word = plan[row, k]
+            tile = tiles[jnp.minimum(lax.shift_right_logical(word, 8), capacity - 1)]
+            own = jnp.minimum(lax.bitwise_and(word, STRIDE - 1), source.shape[0] - 1)
+            return word, source[own], tile
+
         def group(g, total):
-            for u in range(UNROLL):
-                k = g * UNROLL + u
+            for u in range(unroll):
+                k = g * unroll + u
+                word, left, left_tile = pick(2 * k)
+                unused, right, right_tile = pick(2 * k + 1)
                 product = lax.dot_general(
-                    source[block_ref[base + k]],
-                    tiles[order_ref[base + k]],
-                    (dims, ((), ())),
+                    jnp.concatenate([left, right], axis=1),
+                    jnp.concatenate([left_tile, right_tile], axis=dims),
+                    (((1,), (dims,)), ((), ())),
                     preferred_element_type=F32,
                 )
-                total = total * keep_ref[base + k] + product
-                running[k] = total
+                keep = lax.bitwise_and(lax.shift_right_logical(word, 7), 1).astype(F32)
+                total = total * keep + product
+                running[k + 1] = total
             return total
 
-        lax.fori_loop(0, capacity // UNROLL, group, jnp.zeros((channels, block), F32))
-
-    tile_pass(0, extended, ((1,), (1,)))
+        lax.fori_loop(0, GROUPS, group, jnp.zeros((channels, block), F32))
+
+    tile_pass(0, extended, 1)
     for n in range(row_blocks):
         j = n % per_width
-        agg_send[n // per_width, :, j * block : (j + 1) * block] = (
-            running[last_ref[n]] * has_ref[n]
-        ).astype(BF16)
+        agg_send[n // per_width, :, j * block : (j + 1) * block] = closing(1, n).astype(BF16)
     agg_copies = feat_exchange(AGG, agg_send, agg_recv)
     agg_recv[my_feat] = agg_send[my_feat]
     arrived(cot_copies)
@@ -258,22 +356,23 @@
     terms_copies = feat_exchange(TERMS, terms_send, terms_recv)
     terms_recv[my_feat] = terms_send[my_feat]
 
+    grad_blocks[0] = jnp.zeros((channels, block), BF16)
+    rows_col = jnp.broadcast_to(rows.astype(F32), (block, slots)).T[:, :1].astype(jnp.int32)
+
     arrived(grad_copies)
     for n in range(row_blocks):
         j = n % per_width
-        grad_blocks[n] = grad_recv[n // per_width, :, j * block : (j + 1) * block]
-    tile_pass(capacity, grad_blocks, ((1,), (0,)))
+        grad_blocks[n + 1] = grad_recv[n // per_width, :, j * block : (j + 1) * block]
+    tile_pass(2, grad_blocks, 0)
 
     for s in range(row_blocks, src_blocks):
-        value = (running[last_ref[src_blocks + s]] * has_ref[src_blocks + s]).astype(BF16)
+        value = closing(3, s).astype(BF16)
         for h in range(per_block):
             back_send[(s - row_blocks) * per_block + h] = value[:, h * halo : (h + 1) * halo]
     back_copies = vert_exchange(HALO_BACK, back_send, back_recv)
     back_recv[my_vert] = back_send[my_vert]
     for s in range(row_blocks):
-        mixed_grad[:, s * block : (s + 1) * block] = (
-            running[last_ref[src_blocks + s]] * has_ref[src_blocks + s]
-        )
+        mixed_grad[:, s * block : (s + 1) * block] = closing(3, s)
 
     arrived(terms_copies)
     total = terms_recv[0]
@@ -287,7 +386,6 @@
 
     arrived(back_copies)
     returned = jnp.concatenate([back_recv[q] for q in range(vert)], axis=1)
-    rows_col = rows_col_ref[...]
 
     def finish(i, sums):
         start = pl.multiple_of(i * step, step)
@@ -296,9 +394,9 @@
         grad_mixed = mixed_grad[:, pl.ds(start, step)] + jnp.dot(
             returned, onehot, preferred_element_type=F32
         )
+        mixed_grad[:, pl.ds(start, step)] = grad_mixed
         out = []
         for j in range(state_count):
-            grad_states_ref[j, :, pl.ds(start, step)] = (depth[j] * grad_mixed).astype(BF16)
             term = states_ref[j, :, pl.ds(start, step)].astype(F32) * grad_mixed
             term = term[:, :block] + term[:, block:]
             out.append(sums[j] + term)
@@ -309,7 +407,7 @@
         row_count // step,
         finish,
         tuple(jnp.zeros((channels, block), F32) for _ in range(state_count)),
-        unroll=2,
+        unroll=MIX_UNROLL,
     )
     lane = lax.broadcasted_iota(jnp.int32, (channels, block), 1)
     packed = jnp.zeros((channels, block), F32)
@@ -323,12 +421,13 @@
     for q in range(1, vert):
         total += sums_recv[q]
     grad_weight_ref[...] = total[:, :features] * norm_scale
-    grad_bias_ref[...] = total[:, features:] * norm_scale
+    grad_bias_ref[...] = row_of(total[:, features : features + 1] * norm_scale)
     arrived(depth_copies)
     total = depth_recv[0]
     for q in range(1, vert):
         total += depth_recv[q]
-    grad_depth_ref[...] = total * norm_scale
+    for j in range(state_count):
+        grad_depth_ref[j : j + 1, :] = row_of(total[:, j : j + 1] * norm_scale)
     for copies in (
         halo_copies,
         cot_copies,
@@ -345,24 +444,15 @@
             copy.wait_send()
 
 
-def sort_tiles(keys, others, key_count):
-    capacity = keys.shape[1]
-    spot = jnp.arange(capacity, dtype=jnp.int32)
-    full = keys * capacity + spot[None, :]
-    rank = jnp.sum((full[:, None, :] < full[:, :, None]).astype(jnp.int32), axis=2)
-    packed = (spot[None, :] * 128 + keys) * 128 + others
-    chosen = rank[:, None, :] == spot[None, :, None]
-    packed = jnp.sum(jnp.where(chosen, packed[:, None, :], 0), axis=2)
-    order = packed // (128 * 128)
-    sorted_keys = (packed // 128) % 128
-    other = packed % 128
-    before = jnp.concatenate([jnp.full((2, 1), -1, jnp.int32), sorted_keys[:, :-1]], axis=1)
-    keep = (sorted_keys == before).astype(F32)
-    bins = jnp.arange(key_count, dtype=jnp.int32)[None, :, None]
-    upto = jnp.sum((keys[:, None, :] <= bins).astype(jnp.int32), axis=2)
-    has = jnp.any(keys[:, None, :] == bins, axis=2).astype(F32)
-    last = jnp.maximum(upto - 1, 0)
-    return [a.reshape(-1) for a in (order, other, keep, last, has)]
+def output_kernel(
+    layer, mixed_grad, grad_weight, grad_bias, grad_depth, depth_ref, layer_out, states_out, *outs
+):
+    layer_out[...] = layer[...]
+    for ref, out in zip((grad_weight, grad_bias, grad_depth), outs):
+        out[...] = ref[...]
+    for j in range(depth_ref.shape[0]):
+        scale = column_of(depth_ref[j : j + 1, :])
+        states_out[j] = (scale * mixed_grad[...]).astype(BF16)
 
 
 def local(
@@ -388,33 +478,30 @@
     src_blocks = (row_count + slots) // block
     norm_scale = 1.0 / math.sqrt(vert * row_count)
 
-    live = jnp.arange(capacity, dtype=jnp.int32)[None, :] < tile_count[0]
-    both = jnp.concatenate([tile_dst, tile_src], axis=0)
-    keys = jnp.where(live, both, src_blocks)
-    others = jnp.concatenate([tile_src, tile_dst], axis=0)
-    scalars = sort_tiles(keys, others, src_blocks)
-
     vmem = pl.BlockSpec(memory_space=pltpu.VMEM)
     smem = pl.BlockSpec(memory_space=pltpu.SMEM)
     most = max(vert, feat)
     terms = features + block
-    layer, grad_states, grad_weight, grad_bias, grad_depth = pl.pallas_call(
+    hbm = pl.BlockSpec(memory_space=pltpu.HBM)
+    pairs = -(-((capacity + src_blocks) // 2) // GROUPS) * GROUPS
+    lanes = -(-2 * pairs // block) * block
+    layer, mixed_grad, grad_weight, grad_bias, grad_depth = pl.pallas_call(
         functools.partial(
             whole_kernel, (vert, feat, channels, row_count, block, halo), norm_scale
         ),
         out_shape=(
             jax.ShapeDtypeStruct((channels, row_count), BF16),
-            jax.ShapeDtypeStruct((state_count, channels, row_count), BF16),
+            jax.ShapeDtypeStruct((channels, row_count), F32),
             jax.ShapeDtypeStruct((channels, features), F32),
-            jax.ShapeDtypeStruct((channels, block), F32),
-            jax.ShapeDtypeStruct((channels, block), F32),
+            jax.ShapeDtypeStruct((1, channels), F32),
+            jax.ShapeDtypeStruct((state_count, channels), F32),
         ),
-        in_specs=[smem] * 5 + [vmem] * 7 + [pl.BlockSpec(memory_space=pl.ANY)],
+        in_specs=[smem] + [vmem] * 4 + [hbm, vmem] + [hbm] * 3,
         out_specs=(vmem,) * 5,
         scratch_shapes=[
             pltpu.VMEM((capacity, block, block), BF16),
-            pltpu.VMEM((src_blocks, channels, block), BF16),
-            pltpu.VMEM((capacity, channels, block), F32),
+            pltpu.VMEM((src_blocks + 1, channels, block), BF16),
+            pltpu.VMEM((pairs + 1, channels, block), F32),
             pltpu.VMEM((vert, channels, halo), BF16),
             pltpu.VMEM((vert, channels, halo), BF16),
             pltpu.VMEM((vert, channels, halo), BF16),
@@ -431,28 +518,46 @@
             pltpu.VMEM((feat, channels, terms), F32),
             pltpu.VMEM((vert, channels, terms), F32),
             pltpu.VMEM((vert, channels, block), F32),
-            pltpu.VMEM((row_blocks, channels, block), BF16),
-            pltpu.VMEM((channels, row_count), F32),
+            pltpu.VMEM((row_blocks + 1, channels, block), BF16),
             pltpu.VMEM((features, features), BF16),
+            pltpu.VMEM((features, features), BF16),
+            pltpu.VMEM((state_count, channels, row_count), BF16),
+            pltpu.VMEM((8, lanes), jnp.int32),
+            pltpu.SMEM((8, lanes), jnp.int32),
             pltpu.SemaphoreType.DMA((TILE_PARTS,)),
+            pltpu.SemaphoreType.DMA((5,)),
             pltpu.SemaphoreType.DMA((10, most)),
             pltpu.SemaphoreType.DMA((10, most)),
         ],
         compiler_params=pltpu.CompilerParams(
-            collective_id=0, has_side_effects=True, vmem_limit_bytes=48 * 1024 * 1024
+            collective_id=0, has_side_effects=True, vmem_limit_bytes=VMEM_LIMIT
         ),
     )(
-        *scalars,
+        tile_count,
+        tile_dst,
+        tile_src,
+        depth_weight,
+        send_rows,
+        weight,
+        bias_vec[None, :],
         states,
-        depth_weight.T,
-        send_rows.reshape(1, slots),
-        send_rows.reshape(slots, 1),
-        weight,
-        jnp.broadcast_to(bias_vec[:, None], (channels, block)),
         cotangent,
         tile_values,
     )
-    return layer, grad_states, grad_weight, grad_bias[:, 0], grad_depth[:, :state_count].T
+    layer_out, grad_states, grad_weight, grad_bias, grad_depth = pl.pallas_call(
+        output_kernel,
+        out_shape=(
+            jax.ShapeDtypeStruct((channels, row_count), BF16),
+            jax.ShapeDtypeStruct((state_count, channels, row_count), BF16),
+            jax.ShapeDtypeStruct((channels, features), F32),
+            jax.ShapeDtypeStruct((1, channels), F32),
+            jax.ShapeDtypeStruct((state_count, channels), F32),
+        ),
+        in_specs=[vmem] * 6,
+        out_specs=(vmem,) * 5,
+        compiler_params=pltpu.CompilerParams(vmem_limit_bytes=VMEM_LIMIT),
+    )(layer, mixed_grad, grad_weight, grad_bias, grad_depth, depth_weight)
+    return layer_out, grad_states, grad_weight, grad_bias[0], grad_depth
 
 
 def solution(mesh):

time: 58.2 us -> 45.2 us (0.78)
  local copies, waits for them, and re-layouts: 9.88 us -> 0 us
  other arithmetic: 1.53 us -> 0 us
  Pallas kernels: 45.1 us -> 43.7 us
    unnamed x13 -> x0, local copies, waits for them, and re-layouts: 6.78 us -> none
    pallas_call x1, Pallas kernels: 45.1 us -> 41.4 us  [local(): pl.pallas_call(functools.partial(whole_kernel, (vert, feat, channels, row...]
    pallas_call x0 -> x1, Pallas kernels: none -> 2.35 us  [local(): pl.pallas_call(output_kernel, out_shape=(jax.ShapeDtypeStruct((channels,...]
    reshape x2 -> x0, local copies, waits for them, and re-layouts: 1.58 us -> none  [the longest x1 0.82 us: local(): send_rows.reshape(slots, 1)]
    select_n x3 -> x0, other arithmetic: 0.79 us -> none  [the longest x1 0.77 us: local(): keys = jnp.where(live, both, src_blocks)]
    broadcast_in_dim x1 -> x0, local copies, waits for them, and re-layouts: 0.72 us -> none  [local(): jnp.broadcast_to(bias_vec[:, None], (channels, block))]
    slice x1 -> x0, local copies, waits for them, and re-layouts: 0.63 us -> none  [local(): grad_bias[:, 0]]
where the time goes in v2:
time: 45.2 us; the launch traced here: 45 us
  Pallas kernels  43.7 us (97%)
  between operations  1.29 us (3%)
    pallas_call x1, Pallas kernels, local(): pl.pallas_call(functools.partial(whole_kernel, (vert, feat, channels, row...  41.4 us
    pallas_call x1, Pallas kernels, local(): pl.pallas_call(output_kernel, out_shape=(jax.ShapeDtypeStruct((channels,...  2.35 us

profile of v2, /device:TPU:0, one launch (start us, length us, event | category | flops | bytes accessed | tf_op | source)
XLA Modules:
  0.0 45.0 jit_solution(2120698881952362102)
XLA Ops:
  1.3 41.4 %shard_map.137 = (bf16[32,4096]{1,0:T(8,128)(2,1)}, f32[32,4096]{1,0:T(8,128)}, f32[32,256]{1,0:T(8,128)}, f32[1,32]{1,0:T(1,128)}, f32[4,32]{1,0:T(4,128)}) custom-call(s32[1]{0:T(128)S(6)} %copy.15.count_ref, s32[1,256]{1,0:T(1,128)} %dst_ref.1, s32[1,256]{1,0:T(1,128)} %src_ref.1, f32[4,32]{1,0:T(4,128)} %depth_ref.3, s32[1,4,64]{2,1,0:T(4,128)} %rows_ref.1, ...), custom_call_target="tpu_custom_call" | custom-call | tf_op jit(solution)/shard_map/pallas_call | solution.py:488
  42.7 2.4 %shard_map.138 = (bf16[32,4096]{1,0:T(8,128)(2,1)}, bf16[4,32,4096]{2,1,0:T(8,128)(2,1)}, f32[32,256]{1,0:T(8,128)}, f32[1,32]{1,0:T(1,128)}, f32[4,32]{1,0:T(4,128)}) custom-call(bf16[32,4096]{1,0:T(8,128)(2,1)} %get-tuple-element.15.layer, f32[32,4096]{1,0:T(8,128)} %get-tuple-element.16.mixed_grad, f32[32,256]{1,0:T(8,128)} %get-tuple-element.17.grad_weight, ...), custom_call_target="tpu_custom_call" | custom-call | tf_op jit(solution)/shard_map/pallas_call | solution.py:547

commit v3 on v2

--- a/solution.py
+++ b/solution.py
@@ -12,7 +12,8 @@
 BF16 = jnp.bfloat16
 HALO_OUT, COT, BIAS, AGG, GRAD, LAYER, TERMS, HALO_BACK, SUMS, DEPTH = range(10)
 TILE_PARTS = 8
-GROUPS = 6
+GROUP = 10
+REPEAT = 3
 VMEM_LIMIT = 63 * 1024 * 1024
 STRIDE = 128
 MIX_UNROLL = 8
@@ -35,7 +36,7 @@
     return jnp.sum(jnp.where(diagonal(size), spread, 0.0), axis=0, keepdims=True)
 
 
-def plan_tiles(tile_total, dst, src, plan_vec):
+def plan_tiles(tile_total, dst, src, plan_vec, keep_vec):
     capacity = dst.shape[1]
     lanes = plan_vec.shape[1]
     live = lax.broadcasted_iota(jnp.int32, (1, capacity), 1) < tile_total
@@ -54,6 +55,7 @@
     bins = lax.broadcasted_iota(jnp.int32, (capacity, STRIDE), 1).astype(F32)
     spots = lax.broadcasted_iota(jnp.int32, (capacity, lanes), 1).astype(F32)
     plan_vec[...] = jnp.zeros(plan_vec.shape, jnp.int32)
+    keep_vec[...] = jnp.zeros(keep_vec.shape, F32)
     for row, key_row, key, other in (
         (0, dst_key, turned[:, 0:1], turned[:, 3:4]),
         (2, src_key, turned[:, 1:2], turned[:, 2:3]),
@@ -64,7 +66,11 @@
         pairs = jnp.floor((counts + 1.0) * 0.5)
         first = jnp.sum(jnp.where(bins < key, pairs, 0.0), axis=1, keepdims=True)
         spot = jnp.where(key == dead, -1.0, 2.0 * first + inside)
-        word = (2.0 * place + jnp.where(inside > 0.0, 1.0, 0.0)) * STRIDE + other + 1.0
+        word = place * STRIDE + other + 1.0
+        goes_on = jnp.where(inside > 0.0, 1.0, 0.0)
+        keep_vec[row : row + 1, :] = jnp.sum(
+            jnp.where(spots == spot, goes_on, 0.0), axis=0, keepdims=True
+        )
         words = jnp.sum(jnp.where(spots == spot, word, 0.0), axis=0, keepdims=True)
         plan_vec[row : row + 1, :] = words.astype(jnp.int32)
         after = jnp.floor(spot * 0.5) + 1.0
@@ -115,6 +121,9 @@
     states_ref,
     plan_vec,
     plan,
+    keep_vec,
+    keep,
+    picked_states,
     tile_sem,
     local_sem,
     send_sem,
@@ -127,7 +136,6 @@
     features = channels * feat
     row_blocks = row_count // block
     src_blocks = extended.shape[0] - 1
-    unroll = (running.shape[0] - 1) // GROUPS
     slots = vert * halo
     per_block = block // halo
     per_width = width // block
@@ -233,25 +241,38 @@
 
     def mix(i, picked):
         start = pl.multiple_of(i * step, step)
-        total = depth[0] * states_ref[0, :, pl.ds(start, step)].astype(F32)
+        here_states = states_ref[:, :, pl.ds(start, step)]
+        total = depth[0] * here_states[0].astype(F32)
         for j in range(1, state_count):
-            total += depth[j] * states_ref[j, :, pl.ds(start, step)].astype(F32)
+            total += depth[j] * here_states[j].astype(F32)
         mixed = total.astype(BF16)
         extended[2 * i + 1] = mixed[:, :block]
         extended[2 * i + 2] = mixed[:, block:]
         here = lax.broadcasted_iota(jnp.int32, (step, slots), 0) + start
         onehot = jnp.where(here == rows, 1.0, 0.0).astype(BF16)
-        return picked + jnp.dot(mixed, onehot, preferred_element_type=F32)
+        return picked + jnp.dot(
+            here_states.reshape(state_count * channels, step), onehot, preferred_element_type=F32
+        )
 
     steps = row_count // step
     states_copies[0].wait()
     picked = lax.fori_loop(
-        0, steps // 2, mix, jnp.zeros((channels, slots), F32), unroll=MIX_UNROLL
+        0, steps // 2, mix, jnp.zeros((state_count * channels, slots), F32), unroll=MIX_UNROLL
     )
     states_copies[1].wait()
-    picked = lax.fori_loop(steps // 2, steps, mix, picked, unroll=MIX_UNROLL).astype(BF16)
+    picked = lax.fori_loop(steps // 2, steps, mix, picked, unroll=MIX_UNROLL)
+    picked = picked.reshape(state_count, channels, slots)
+    listed = depth[0] * picked[0]
+    for j in range(1, state_count):
+        listed += depth[j] * picked[j]
+    listed = listed.astype(BF16)
+    picked_states[...] = picked
+
+    def widened(part):
+        return jnp.concatenate([part] * per_block, axis=1)
+
     for p in range(vert):
-        halo_send[p] = picked[:, p * halo : (p + 1) * halo]
+        halo_send[p] = widened(listed[:, p * halo : (p + 1) * halo])
 
     pl.semaphore_wait(barrier, vert + feat - 2)
     halo_copies = vert_exchange(HALO_OUT, halo_send, halo_recv)
@@ -271,9 +292,11 @@
     for copy in cot_copies + bias_copies:
         copy.start()
     halo_recv[my_vert] = halo_send[my_vert]
-    plan_tiles(count_ref[0], dst_ref[...], src_ref[...], plan_vec)
+    plan_tiles(count_ref[0], dst_ref[...], src_ref[...], plan_vec, keep_vec)
     plan_copy = pltpu.make_async_copy(plan_vec, plan, local_sem.at[4])
     plan_copy.start()
+    keep_copy = pltpu.make_async_copy(keep_vec, keep, local_sem.at[5])
+    keep_copy.start()
     weight_copy.wait()
     own_cot.wait()
     weight = weight_ref[...]
@@ -282,12 +305,13 @@
     arrived(halo_copies)
     for j in range(src_blocks - row_blocks):
         extended[row_blocks + j + 1] = jnp.concatenate(
-            [halo_recv[j * per_block + h] for h in range(per_block)], axis=1
+            [halo_recv[j * per_block + h, :, :halo] for h in range(per_block)], axis=1
         )
     for copy in tile_copies:
         copy.wait()
 
     plan_copy.wait()
+    keep_copy.wait()
 
     def closing(row, n):
         return running[jnp.clip(plan[row, n], 0, running.shape[0] - 1)]
@@ -295,27 +319,37 @@
     def tile_pass(row, source, dims):
         def pick(k):
             word = plan[row, k]
-            tile = tiles[jnp.minimum(lax.shift_right_logical(word, 8), capacity - 1)]
+            tile = tiles[jnp.minimum(lax.shift_right_logical(word, 7), capacity - 1)]
             own = jnp.minimum(lax.bitwise_and(word, STRIDE - 1), source.shape[0] - 1)
-            return word, source[own], tile
+            return source[own], tile
 
         def group(g, total):
-            for u in range(unroll):
-                k = g * unroll + u
-                word, left, left_tile = pick(2 * k)
-                unused, right, right_tile = pick(2 * k + 1)
-                product = lax.dot_general(
-                    jnp.concatenate([left, right], axis=1),
-                    jnp.concatenate([left_tile, right_tile], axis=dims),
-                    (((1,), (dims,)), ((), ())),
-                    preferred_element_type=F32,
+            products = []
+            for u in range(GROUP):
+                k = g * GROUP + u
+                left, left_tile = pick(2 * k)
+                right, right_tile = pick(2 * k + 1)
+                products.append(
+                    lax.dot_general(
+                        jnp.concatenate([left, right], axis=1),
+                        jnp.concatenate([left_tile, right_tile], axis=dims),
+                        (((1,), (dims,)), ((), ())),
+                        preferred_element_type=F32,
+                    )
                 )
-                keep = lax.bitwise_and(lax.shift_right_logical(word, 7), 1).astype(F32)
-                total = total * keep + product
+            for u in range(GROUP):
+                k = g * GROUP + u
+                total = total * keep[row, 2 * k] + products[u]
                 running[k + 1] = total
             return total
 
-        lax.fori_loop(0, GROUPS, group, jnp.zeros((channels, block), F32))
+        lax.fori_loop(
+            0,
+            (running.shape[0] - 1) // GROUP,
+            group,
+            jnp.zeros((channels, block), F32),
+            unroll=REPEAT,
+        )
 
     tile_pass(0, extended, 1)
     for n in range(row_blocks):
@@ -368,11 +402,42 @@
     for s in range(row_blocks, src_blocks):
         value = closing(3, s).astype(BF16)
         for h in range(per_block):
-            back_send[(s - row_blocks) * per_block + h] = value[:, h * halo : (h + 1) * halo]
+            back_send[(s - row_blocks) * per_block + h] = widened(
+                value[:, h * halo : (h + 1) * halo]
+            )
     back_copies = vert_exchange(HALO_BACK, back_send, back_recv)
     back_recv[my_vert] = back_send[my_vert]
     for s in range(row_blocks):
         mixed_grad[:, s * block : (s + 1) * block] = closing(3, s)
+
+    def own_sums(i, sums):
+        start = pl.multiple_of(i * step, step)
+        own = mixed_grad[:, pl.ds(start, step)]
+        out = []
+        for j in range(state_count):
+            term = states_ref[j, :, pl.ds(start, step)].astype(F32) * own
+            out.append(sums[j] + term[:, :block] + term[:, block:])
+        return tuple(out)
+
+    sums = lax.fori_loop(
+        0,
+        steps,
+        own_sums,
+        tuple(jnp.zeros((channels, block), F32) for _ in range(state_count)),
+        unroll=4,
+    )
+    own_depth = [jnp.sum(part, axis=1, keepdims=True) for part in sums]
+
+    arrived(back_copies)
+    returned = jnp.concatenate([back_recv[q, :, :halo] for q in range(vert)], axis=1)
+    returned32 = returned.astype(F32)
+    lane = lax.broadcasted_iota(jnp.int32, (channels, block), 1)
+    packed = jnp.zeros((channels, block), F32)
+    for j in range(state_count):
+        listed_sum = jnp.sum(picked_states[j] * returned32, axis=1, keepdims=True)
+        packed = jnp.where(lane == j, own_depth[j] + listed_sum, packed)
+    depth_recv[my_vert] = packed
+    depth_copies = vert_spread(DEPTH, depth_recv)
 
     arrived(terms_copies)
     total = terms_recv[0]
@@ -380,41 +445,20 @@
         total += terms_recv[f]
     sums_recv[my_vert] = total
     sums_copies = vert_spread(SUMS, sums_recv)
+
+    def finish(i, carry):
+        start = pl.multiple_of(i * step, step)
+        here = lax.broadcasted_iota(jnp.int32, (slots, step), 1) + start
+        onehot = jnp.where(here == rows_col, 1.0, 0.0).astype(BF16)
+        mixed_grad[:, pl.ds(start, step)] += jnp.dot(
+            returned, onehot, preferred_element_type=F32
+        )
+        return carry
+
+    lax.fori_loop(0, steps, finish, 0, unroll=MIX_UNROLL)
     arrived(layer_copies)
     for f in range(feat):
         layer_ref[:, f * width : (f + 1) * width] = layer_recv[f]
-
-    arrived(back_copies)
-    returned = jnp.concatenate([back_recv[q] for q in range(vert)], axis=1)
-
-    def finish(i, sums):
-        start = pl.multiple_of(i * step, step)
-        here = lax.broadcasted_iota(jnp.int32, (slots, step), 1) + start
-        onehot = jnp.where(here == rows_col, 1.0, 0.0).astype(BF16)
-        grad_mixed = mixed_grad[:, pl.ds(start, step)] + jnp.dot(
-            returned, onehot, preferred_element_type=F32
-        )
-        mixed_grad[:, pl.ds(start, step)] = grad_mixed
-        out = []
-        for j in range(state_count):
-            term = states_ref[j, :, pl.ds(start, step)].astype(F32) * grad_mixed
-            term = term[:, :block] + term[:, block:]
-            out.append(sums[j] + term)
-        return tuple(out)
-
-    sums = lax.fori_loop(
-        0,
-        row_count // step,
-        finish,
-        tuple(jnp.zeros((channels, block), F32) for _ in range(state_count)),
-        unroll=MIX_UNROLL,
-    )
-    lane = lax.broadcasted_iota(jnp.int32, (channels, block), 1)
-    packed = jnp.zeros((channels, block), F32)
-    for j in range(state_count):
-        packed = jnp.where(lane == j, jnp.sum(sums[j], axis=1, keepdims=True), packed)
-    depth_recv[my_vert] = packed
-    depth_copies = vert_spread(DEPTH, depth_recv)
 
     arrived(sums_copies)
     total = sums_recv[0]
@@ -483,7 +527,7 @@
     most = max(vert, feat)
     terms = features + block
     hbm = pl.BlockSpec(memory_space=pltpu.HBM)
-    pairs = -(-((capacity + src_blocks) // 2) // GROUPS) * GROUPS
+    pairs = -(-((capacity + src_blocks) // 2) // GROUP) * GROUP
     lanes = -(-2 * pairs // block) * block
     layer, mixed_grad, grad_weight, grad_bias, grad_depth = pl.pallas_call(
         functools.partial(
@@ -502,10 +546,10 @@
             pltpu.VMEM((capacity, block, block), BF16),
             pltpu.VMEM((src_blocks + 1, channels, block), BF16),
             pltpu.VMEM((pairs + 1, channels, block), F32),
-            pltpu.VMEM((vert, channels, halo), BF16),
-            pltpu.VMEM((vert, channels, halo), BF16),
-            pltpu.VMEM((vert, channels, halo), BF16),
-            pltpu.VMEM((vert, channels, halo), BF16),
+            pltpu.VMEM((vert, channels, block), BF16),
+            pltpu.VMEM((vert, channels, block), BF16),
+            pltpu.VMEM((vert, channels, block), BF16),
+            pltpu.VMEM((vert, channels, block), BF16),
             pltpu.VMEM((feat, channels, width), BF16),
             pltpu.VMEM((feat, channels, block), F32),
             pltpu.VMEM((feat, channels, width), BF16),
@@ -524,8 +568,11 @@
             pltpu.VMEM((state_count, channels, row_count), BF16),
             pltpu.VMEM((8, lanes), jnp.int32),
             pltpu.SMEM((8, lanes), jnp.int32),
+            pltpu.VMEM((8, lanes), F32),
+            pltpu.SMEM((8, lanes), F32),
+            pltpu.VMEM((state_count, channels, slots), F32),
             pltpu.SemaphoreType.DMA((TILE_PARTS,)),
-            pltpu.SemaphoreType.DMA((5,)),
+            pltpu.SemaphoreType.DMA((6,)),
             pltpu.SemaphoreType.DMA((10, most)),
             pltpu.SemaphoreType.DMA((10, most)),
         ],

time: 45.2 us -> 44.2 us (0.978)
  Pallas kernels: 43.7 us -> 42.8 us
    pallas_call x1, Pallas kernels: 41.4 us -> 40.4 us  [local(): pl.pallas_call(functools.partial(whole_kernel, (vert, feat, channels, row...]
where the time goes in v3:
time: 44.2 us; the launch traced here: 44.1 us
  Pallas kernels  42.8 us (97%)
  between operations  1.29 us (3%)
    pallas_call x1, Pallas kernels, local(): pl.pallas_call(functools.partial(whole_kernel, (vert, feat, channels, row...  40.4 us
    pallas_call x1, Pallas kernels, local(): pl.pallas_call(output_kernel, out_shape=(jax.ShapeDtypeStruct((channels,...  2.35 us

profile of v3, /device:TPU:0, one launch (start us, length us, event | category | flops | bytes accessed | tf_op | source)
XLA Modules:
  0.0 44.1 jit_solution(14782645987208413981)
XLA Ops:
  1.3 40.4 %shard_map.137 = (bf16[32,4096]{1,0:T(8,128)(2,1)}, f32[32,4096]{1,0:T(8,128)}, f32[32,256]{1,0:T(8,128)}, f32[1,32]{1,0:T(1,128)}, f32[4,32]{1,0:T(4,128)}) custom-call(s32[1]{0:T(128)S(6)} %copy.15.count_ref, s32[1,256]{1,0:T(1,128)} %dst_ref.1, s32[1,256]{1,0:T(1,128)} %src_ref.1, f32[4,32]{1,0:T(4,128)} %depth_ref.3, s32[1,4,64]{2,1,0:T(4,128)} %rows_ref.1, ...), custom_call_target="tpu_custom_call" | custom-call | tf_op jit(solution)/shard_map/pallas_call | solution.py:532
  41.7 2.4 %shard_map.138 = (bf16[32,4096]{1,0:T(8,128)(2,1)}, bf16[4,32,4096]{2,1,0:T(8,128)(2,1)}, f32[32,256]{1,0:T(8,128)}, f32[1,32]{1,0:T(1,128)}, f32[4,32]{1,0:T(4,128)}) custom-call(bf16[32,4096]{1,0:T(8,128)(2,1)} %get-tuple-element.15.layer, f32[32,4096]{1,0:T(8,128)} %get-tuple-element.16.mixed_grad, f32[32,256]{1,0:T(8,128)} %get-tuple-element.17.grad_weight, ...), custom_call_target="tpu_custom_call" | custom-call | tf_op jit(solution)/shard_map/pallas_call | solution.py:594

commit v4 on v3

--- a/solution.py
+++ b/solution.py
@@ -325,18 +325,31 @@
 
         def group(g, total):
             products = []
-            for u in range(GROUP):
-                k = g * GROUP + u
-                left, left_tile = pick(2 * k)
-                right, right_tile = pick(2 * k + 1)
-                products.append(
-                    lax.dot_general(
-                        jnp.concatenate([left, right], axis=1),
-                        jnp.concatenate([left_tile, right_tile], axis=dims),
-                        (((1,), (dims,)), ((), ())),
-                        preferred_element_type=F32,
-                    )
+            for u in range(0, GROUP, 2):
+                k = 2 * (g * GROUP + u)
+                sources, parts = zip(*[pick(k + i) for i in range(4)])
+                rows_now = jnp.concatenate(
+                    [
+                        jnp.concatenate(sources[:2], axis=1),
+                        jnp.concatenate(sources[2:], axis=1),
+                    ],
+                    axis=0,
                 )
+                tiles_now = jnp.concatenate(
+                    [
+                        jnp.concatenate(parts[:2], axis=dims),
+                        jnp.concatenate(parts[2:], axis=dims),
+                    ],
+                    axis=1 - dims,
+                )
+                product = lax.dot_general(
+                    rows_now,
+                    tiles_now,
+                    (((1,), (dims,)), ((), ())),
+                    preferred_element_type=F32,
+                )
+                products.append(product[:channels, :block])
+                products.append(product[channels:, block:])
             for u in range(GROUP):
                 k = g * GROUP + u
                 total = total * keep[row, 2 * k] + products[u]
@@ -410,6 +423,13 @@
     for s in range(row_blocks):
         mixed_grad[:, s * block : (s + 1) * block] = closing(3, s)
 
+    arrived(terms_copies)
+    total = terms_recv[0]
+    for f in range(1, feat):
+        total += terms_recv[f]
+    sums_recv[my_vert] = total
+    sums_copies = vert_spread(SUMS, sums_recv)
+
     def own_sums(i, sums):
         start = pl.multiple_of(i * step, step)
         own = mixed_grad[:, pl.ds(start, step)]
@@ -438,13 +458,6 @@
         packed = jnp.where(lane == j, own_depth[j] + listed_sum, packed)
     depth_recv[my_vert] = packed
     depth_copies = vert_spread(DEPTH, depth_recv)
-
-    arrived(terms_copies)
-    total = terms_recv[0]
-    for f in range(1, feat):
-        total += terms_recv[f]
-    sums_recv[my_vert] = total
-    sums_copies = vert_spread(SUMS, sums_recv)
 
     def finish(i, carry):
         start = pl.multiple_of(i * step, step)

time: 44.2 us -> 45.1 us (1.020)
  Pallas kernels: 42.8 us -> 43.6 us
    pallas_call x1, Pallas kernels: 40.4 us -> 41.2 us  [local(): pl.pallas_call(functools.partial(whole_kernel, (vert, feat, channels, row...]
where the time goes in v4:
time: 45.1 us; the launch traced here: 44.9 us
  Pallas kernels  43.6 us (97%)
  between operations  1.29 us (3%)
    pallas_call x1, Pallas kernels, local(): pl.pallas_call(functools.partial(whole_kernel, (vert, feat, channels, row...  41.2 us
    pallas_call x1, Pallas kernels, local(): pl.pallas_call(output_kernel, out_shape=(jax.ShapeDtypeStruct((channels,...  2.35 us

profile of v4, /device:TPU:0, one launch (start us, length us, event | category | flops | bytes accessed | tf_op | source)
XLA Modules:
  0.0 44.9 jit_solution(14121789405781499312)
XLA Ops:
  1.3 41.2 %shard_map.137 = (bf16[32,4096]{1,0:T(8,128)(2,1)}, f32[32,4096]{1,0:T(8,128)}, f32[32,256]{1,0:T(8,128)}, f32[1,32]{1,0:T(1,128)}, f32[4,32]{1,0:T(4,128)}) custom-call(s32[1]{0:T(128)S(6)} %copy.15.count_ref, s32[1,256]{1,0:T(1,128)} %dst_ref.1, s32[1,256]{1,0:T(1,128)} %src_ref.1, f32[4,32]{1,0:T(4,128)} %depth_ref.3, s32[1,4,64]{2,1,0:T(4,128)} %rows_ref.1, ...), custom_call_target="tpu_custom_call" | custom-call | tf_op jit(solution)/shard_map/pallas_call | solution.py:545
  42.5 2.4 %shard_map.138 = (bf16[32,4096]{1,0:T(8,128)(2,1)}, bf16[4,32,4096]{2,1,0:T(8,128)(2,1)}, f32[32,256]{1,0:T(8,128)}, f32[1,32]{1,0:T(1,128)}, f32[4,32]{1,0:T(4,128)}) custom-call(bf16[32,4096]{1,0:T(8,128)(2,1)} %get-tuple-element.15.layer, f32[32,4096]{1,0:T(8,128)} %get-tuple-element.16.mixed_grad, f32[32,256]{1,0:T(8,128)} %get-tuple-element.17.grad_weight, ...), custom_call_target="tpu_custom_call" | custom-call | tf_op jit(solution)/shard_map/pallas_call | solution.py:607

commit v5 on v3

--- a/solution.py
+++ b/solution.py
@@ -10,7 +10,7 @@
 
 F32 = jnp.float32
 BF16 = jnp.bfloat16
-HALO_OUT, COT, BIAS, AGG, GRAD, LAYER, TERMS, HALO_BACK, SUMS, DEPTH = range(10)
+HALO_OUT, COT, BIAS, LAYER, TERMS, HALO_BACK, SUMS, DEPTH, AGG, AGG_B, GRAD, GRAD_B = range(12)
 TILE_PARTS = 8
 GROUP = 10
 REPEAT = 3
@@ -139,6 +139,14 @@
     slots = vert * halo
     per_block = block // halo
     per_width = width // block
+    parts, part_width = agg_send.shape[0], agg_send.shape[3]
+    per_part = part_width // block
+
+    def spot_of(n):
+        j = n % per_width
+        start = (j % per_part) * block
+        return j // per_part, n // per_width, slice(start, start + block)
+
     my_vert = lax.axis_index("vert")
     my_feat = lax.axis_index("feat")
 
@@ -316,7 +324,7 @@
     def closing(row, n):
         return running[jnp.clip(plan[row, n], 0, running.shape[0] - 1)]
 
-    def tile_pass(row, source, dims):
+    def tile_pass(row, source, dims, between):
         def pick(k):
             word = plan[row, k]
             tile = tiles[jnp.minimum(lax.shift_right_logical(word, 7), capacity - 1)]
@@ -343,61 +351,91 @@
                 running[k + 1] = total
             return total
 
-        lax.fori_loop(
-            0,
-            (running.shape[0] - 1) // GROUP,
-            group,
-            jnp.zeros((channels, block), F32),
-            unroll=REPEAT,
-        )
-
-    tile_pass(0, extended, 1)
+        groups = (running.shape[0] - 1) // GROUP
+        total = jnp.zeros((channels, block), F32)
+        if between is None:
+            lax.fori_loop(0, groups, group, total, unroll=REPEAT)
+        else:
+            middle = groups * 3 // 5
+            total = lax.fori_loop(0, middle, group, total, unroll=REPEAT)
+            between()
+            lax.fori_loop(middle, groups, group, total, unroll=REPEAT)
+
+    tile_pass(0, extended, 1, None)
     for n in range(row_blocks):
-        j = n % per_width
-        agg_send[n // per_width, :, j * block : (j + 1) * block] = closing(1, n).astype(BF16)
-    agg_copies = feat_exchange(AGG, agg_send, agg_recv)
-    agg_recv[my_feat] = agg_send[my_feat]
+        part, f, columns = spot_of(n)
+        agg_send[part, f, :, columns] = closing(1, n).astype(BF16)
+    agg_copies = [
+        feat_exchange((AGG, AGG_B)[part], agg_send.at[part], agg_recv.at[part])
+        for part in range(parts)
+    ]
+    for part in range(parts):
+        agg_recv[part, my_feat] = agg_send[part, my_feat]
     arrived(cot_copies)
     arrived(bias_copies)
-    arrived(agg_copies)
-
-    aggregated = agg_recv[...].reshape(features, width)
     bias = bias_recv[...].reshape(features, block)[:, :1]
-    pre_act = jnp.dot(weight_t[...], aggregated, preferred_element_type=F32) + bias
-    sigmoid_pre = jax.nn.sigmoid(pre_act)
-    grad_pre32 = (
-        cot_recv[...].reshape(features, width).astype(F32)
-        * sigmoid_pre
-        * (1.0 + pre_act * (1.0 - sigmoid_pre))
-    )
-    grad_pre = grad_pre32.astype(BF16)
-    grad_send[...] = (
-        jnp.dot(weight, grad_pre, preferred_element_type=F32)
-        .astype(BF16)
-        .reshape(feat, channels, width)
-    )
-    grad_copies = feat_exchange(GRAD, grad_send, grad_recv)
-    grad_recv[my_feat] = grad_send[my_feat]
-    layer_send[...] = (pre_act * sigmoid_pre).astype(BF16).reshape(feat, channels, width)
+
+    grad_copies = []
+    pieces = []
+    for part in range(parts):
+        columns = slice(part * part_width, (part + 1) * part_width)
+        arrived(agg_copies[part])
+        aggregated = agg_recv[part].reshape(features, part_width)
+        pre_act = jnp.dot(weight_t[...], aggregated, preferred_element_type=F32) + bias
+        sigmoid_pre = jax.nn.sigmoid(pre_act)
+        grad_pre = (
+            cot_recv[:, :, columns].reshape(features, part_width).astype(F32)
+            * sigmoid_pre
+            * (1.0 + pre_act * (1.0 - sigmoid_pre))
+        ).astype(BF16)
+        grad_send[part] = (
+            jnp.dot(weight, grad_pre, preferred_element_type=F32)
+            .astype(BF16)
+            .reshape(feat, channels, part_width)
+        )
+        grad_copies.append(
+            feat_exchange((GRAD, GRAD_B)[part], grad_send.at[part], grad_recv.at[part])
+        )
+        grad_recv[part, my_feat] = grad_send[part, my_feat]
+        layer_send[:, :, columns] = (
+            (pre_act * sigmoid_pre).astype(BF16).reshape(feat, channels, part_width)
+        )
+        pieces.append((aggregated, grad_pre))
+    weight_terms = jnp.zeros((features, features), F32)
+    bias_terms = jnp.zeros((features, 1), F32)
+    for aggregated, grad_pre in pieces:
+        weight_terms += lax.dot_general(
+            aggregated, grad_pre, (((1,), (1,)), ((), ())), preferred_element_type=F32
+        )
+        bias_terms += jnp.sum(grad_pre.astype(F32), axis=1, keepdims=True)
+    terms_send[:, :, :features] = weight_terms.astype(BF16).reshape(feat, channels, features)
+    terms_send[:, :, features:] = (
+        jnp.broadcast_to(bias_terms, (features, block)).astype(BF16).reshape(feat, channels, block)
+    )
+    terms_copies = feat_exchange(TERMS, terms_send, terms_recv)
+    terms_recv[my_feat] = terms_send[my_feat]
     layer_copies = feat_exchange(LAYER, layer_send, layer_recv)
     layer_recv[my_feat] = layer_send[my_feat]
-    terms_send[:, :, :features] = lax.dot_general(
-        aggregated, grad_pre, (((1,), (1,)), ((), ())), preferred_element_type=F32
-    ).reshape(feat, channels, features)
-    terms_send[:, :, features:] = jnp.broadcast_to(
-        jnp.sum(grad_pre.astype(F32), axis=1, keepdims=True), (features, block)
-    ).reshape(feat, channels, block)
-    terms_copies = feat_exchange(TERMS, terms_send, terms_recv)
-    terms_recv[my_feat] = terms_send[my_feat]
 
     grad_blocks[0] = jnp.zeros((channels, block), BF16)
     rows_col = jnp.broadcast_to(rows.astype(F32), (block, slots)).T[:, :1].astype(jnp.int32)
 
-    arrived(grad_copies)
+    for copies in grad_copies:
+        arrived(copies)
     for n in range(row_blocks):
-        j = n % per_width
-        grad_blocks[n + 1] = grad_recv[n // per_width, :, j * block : (j + 1) * block]
-    tile_pass(2, grad_blocks, 0)
+        part, f, columns = spot_of(n)
+        grad_blocks[n + 1] = grad_recv[part, f, :, columns]
+    sums_copies = []
+
+    def send_sums():
+        arrived(terms_copies)
+        total = terms_recv[0].astype(F32)
+        for f in range(1, feat):
+            total += terms_recv[f].astype(F32)
+        sums_recv[my_vert] = total
+        sums_copies.extend(vert_spread(SUMS, sums_recv))
+
+    tile_pass(2, grad_blocks, 0, send_sums)
 
     for s in range(row_blocks, src_blocks):
         value = closing(3, s).astype(BF16)
@@ -431,20 +469,11 @@
     arrived(back_copies)
     returned = jnp.concatenate([back_recv[q, :, :halo] for q in range(vert)], axis=1)
     returned32 = returned.astype(F32)
-    lane = lax.broadcasted_iota(jnp.int32, (channels, block), 1)
-    packed = jnp.zeros((channels, block), F32)
+    depth_recv[my_vert] = jnp.zeros(depth_recv.shape[1:], F32)
     for j in range(state_count):
         listed_sum = jnp.sum(picked_states[j] * returned32, axis=1, keepdims=True)
-        packed = jnp.where(lane == j, own_depth[j] + listed_sum, packed)
-    depth_recv[my_vert] = packed
+        depth_recv[my_vert, j : j + 1, :channels] = row_of(own_depth[j] + listed_sum)
     depth_copies = vert_spread(DEPTH, depth_recv)
-
-    arrived(terms_copies)
-    total = terms_recv[0]
-    for f in range(1, feat):
-        total += terms_recv[f]
-    sums_recv[my_vert] = total
-    sums_copies = vert_spread(SUMS, sums_recv)
 
     def finish(i, carry):
         start = pl.multiple_of(i * step, step)
@@ -470,14 +499,13 @@
     total = depth_recv[0]
     for q in range(1, vert):
         total += depth_recv[q]
-    for j in range(state_count):
-        grad_depth_ref[j : j + 1, :] = row_of(total[:, j : j + 1] * norm_scale)
+    grad_depth_ref[...] = total[:state_count, :channels] * norm_scale
     for copies in (
         halo_copies,
         cot_copies,
         bias_copies,
-        agg_copies,
-        grad_copies,
+        *agg_copies,
+        *grad_copies,
         layer_copies,
         terms_copies,
         back_copies,
@@ -526,6 +554,7 @@
     smem = pl.BlockSpec(memory_space=pltpu.SMEM)
     most = max(vert, feat)
     terms = features + block
+    parts = 2 if width % (2 * block) == 0 else 1
     hbm = pl.BlockSpec(memory_space=pltpu.HBM)
     pairs = -(-((capacity + src_blocks) // 2) // GROUP) * GROUP
     lanes = -(-2 * pairs // block) * block
@@ -552,16 +581,16 @@
             pltpu.VMEM((vert, channels, block), BF16),
             pltpu.VMEM((feat, channels, width), BF16),
             pltpu.VMEM((feat, channels, block), F32),
+            pltpu.VMEM((parts, feat, channels, width // parts), BF16),
+            pltpu.VMEM((parts, feat, channels, width // parts), BF16),
+            pltpu.VMEM((parts, feat, channels, width // parts), BF16),
+            pltpu.VMEM((parts, feat, channels, width // parts), BF16),
             pltpu.VMEM((feat, channels, width), BF16),
             pltpu.VMEM((feat, channels, width), BF16),
-            pltpu.VMEM((feat, channels, width), BF16),
-            pltpu.VMEM((feat, channels, width), BF16),
-            pltpu.VMEM((feat, channels, width), BF16),
-            pltpu.VMEM((feat, channels, width), BF16),
-            pltpu.VMEM((feat, channels, terms), F32),
-            pltpu.VMEM((feat, channels, terms), F32),
+            pltpu.VMEM((feat, channels, terms), BF16),
+            pltpu.VMEM((feat, channels, terms), BF16),
             pltpu.VMEM((vert, channels, terms), F32),
-            pltpu.VMEM((vert, channels, block), F32),
+            pltpu.VMEM((vert, 8 * -(-state_count // 8), block), F32),
             pltpu.VMEM((row_blocks + 1, channels, block), BF16),
             pltpu.VMEM((features, features), BF16),
             pltpu.VMEM((features, features), BF16),
@@ -573,8 +602,8 @@
             pltpu.VMEM((state_count, channels, slots), F32),
             pltpu.SemaphoreType.DMA((TILE_PARTS,)),
             pltpu.SemaphoreType.DMA((6,)),
-            pltpu.SemaphoreType.DMA((10, most)),
-            pltpu.SemaphoreType.DMA((10, most)),
+            pltpu.SemaphoreType.DMA((12, most)),
+            pltpu.SemaphoreType.DMA((12, most)),
         ],
         compiler_params=pltpu.CompilerParams(
             collective_id=0, has_side_effects=True, vmem_limit_bytes=VMEM_LIMIT

time: 44.2 us -> 43 us (0.973)
  Pallas kernels: 42.8 us -> 41.5 us
    pallas_call x1, Pallas kernels: 40.4 us -> 39.2 us  [local(): pl.pallas_call(functools.partial(whole_kernel, (vert, feat, channels, row...]
where the time goes in v5:
time: 43 us; the launch traced here: 42.8 us
  Pallas kernels  41.5 us (97%)
  between operations  1.29 us (3%)
    pallas_call x1, Pallas kernels, local(): pl.pallas_call(functools.partial(whole_kernel, (vert, feat, channels, row...  39.2 us
    pallas_call x1, Pallas kernels, local(): pl.pallas_call(output_kernel, out_shape=(jax.ShapeDtypeStruct((channels,...  2.35 us

profile of v5, /device:TPU:0, one launch (start us, length us, event | category | flops | bytes accessed | tf_op | source)
XLA Modules:
  0.0 42.8 jit_solution(2058529809151541604)
XLA Ops:
  1.3 39.2 %shard_map.137 = (bf16[32,4096]{1,0:T(8,128)(2,1)}, f32[32,4096]{1,0:T(8,128)}, f32[32,256]{1,0:T(8,128)}, f32[1,32]{1,0:T(1,128)}, f32[4,32]{1,0:T(4,128)}) custom-call(s32[1]{0:T(128)S(6)} %copy.15.count_ref, s32[1,256]{1,0:T(1,128)} %dst_ref.1, s32[1,256]{1,0:T(1,128)} %src_ref.1, f32[4,32]{1,0:T(4,128)} %depth_ref.3, s32[1,4,64]{2,1,0:T(4,128)} %rows_ref.1, ...), custom_call_target="tpu_custom_call" | custom-call | tf_op jit(solution)/shard_map/pallas_call | solution.py:561
  40.5 2.4 %shard_map.138 = (bf16[32,4096]{1,0:T(8,128)(2,1)}, bf16[4,32,4096]{2,1,0:T(8,128)(2,1)}, f32[32,256]{1,0:T(8,128)}, f32[1,32]{1,0:T(1,128)}, f32[4,32]{1,0:T(4,128)}) custom-call(bf16[32,4096]{1,0:T(8,128)(2,1)} %get-tuple-element.15.layer, f32[32,4096]{1,0:T(8,128)} %get-tuple-element.16.mixed_grad, f32[32,256]{1,0:T(8,128)} %get-tuple-element.17.grad_weight, ...), custom_call_target="tpu_custom_call" | custom-call | tf_op jit(solution)/shard_map/pallas_call | solution.py:623

commit v6 on v5

--- a/solution.py
+++ b/solution.py
@@ -13,6 +13,7 @@
 HALO_OUT, COT, BIAS, LAYER, TERMS, HALO_BACK, SUMS, DEPTH, AGG, AGG_B, GRAD, GRAD_B = range(12)
 TILE_PARTS = 8
 GROUP = 10
+OUT_STEPS = 4
 REPEAT = 3
 VMEM_LIMIT = 63 * 1024 * 1024
 STRIDE = 128
@@ -91,8 +92,8 @@
     states_hbm,
     cot_hbm,
     tiles_hbm,
-    layer_ref,
-    mixed_grad,
+    layer_hbm,
+    mixed_hbm,
     grad_weight_ref,
     grad_bias_ref,
     grad_depth_ref,
@@ -124,6 +125,8 @@
     keep_vec,
     keep,
     picked_states,
+    layer_ref,
+    mixed_grad,
     tile_sem,
     local_sem,
     send_sem,
@@ -485,9 +488,13 @@
         return carry
 
     lax.fori_loop(0, steps, finish, 0, unroll=MIX_UNROLL)
+    mixed_out = pltpu.make_async_copy(mixed_grad, mixed_hbm, local_sem.at[6])
+    mixed_out.start()
     arrived(layer_copies)
     for f in range(feat):
         layer_ref[:, f * width : (f + 1) * width] = layer_recv[f]
+    layer_out = pltpu.make_async_copy(layer_ref, layer_hbm, local_sem.at[7])
+    layer_out.start()
 
     arrived(sums_copies)
     total = sums_recv[0]
@@ -500,6 +507,8 @@
     for q in range(1, vert):
         total += depth_recv[q]
     grad_depth_ref[...] = total[:state_count, :channels] * norm_scale
+    mixed_out.wait()
+    layer_out.wait()
     for copies in (
         halo_copies,
         cot_copies,
@@ -570,7 +579,7 @@
             jax.ShapeDtypeStruct((state_count, channels), F32),
         ),
         in_specs=[smem] + [vmem] * 4 + [hbm, vmem] + [hbm] * 3,
-        out_specs=(vmem,) * 5,
+        out_specs=(hbm, hbm, vmem, vmem, vmem),
         scratch_shapes=[
             pltpu.VMEM((capacity, block, block), BF16),
             pltpu.VMEM((src_blocks + 1, channels, block), BF16),
@@ -600,8 +609,10 @@
             pltpu.VMEM((8, lanes), F32),
             pltpu.SMEM((8, lanes), F32),
             pltpu.VMEM((state_count, channels, slots), F32),
+            pltpu.VMEM((channels, row_count), BF16),
+            pltpu.VMEM((channels, row_count), F32),
             pltpu.SemaphoreType.DMA((TILE_PARTS,)),
-            pltpu.SemaphoreType.DMA((6,)),
+            pltpu.SemaphoreType.DMA((8,)),
             pltpu.SemaphoreType.DMA((12, most)),
             pltpu.SemaphoreType.DMA((12, most)),
         ],
@@ -620,6 +631,12 @@
         cotangent,
         tile_values,
     )
+
+    def still(shape):
+        return pl.BlockSpec(shape, lambda i: (0, 0))
+
+    moving = pl.BlockSpec((channels, row_count // OUT_STEPS), lambda i: (0, i))
+    small = [still((channels, features)), still((1, channels)), still((state_count, channels))]
     layer_out, grad_states, grad_weight, grad_bias, grad_depth = pl.pallas_call(
         output_kernel,
         out_shape=(
@@ -629,8 +646,13 @@
             jax.ShapeDtypeStruct((1, channels), F32),
             jax.ShapeDtypeStruct((state_count, channels), F32),
         ),
-        in_specs=[vmem] * 6,
-        out_specs=(vmem,) * 5,
+        grid=(OUT_STEPS,),
+        in_specs=[moving, moving, *small, still(depth_weight.shape)],
+        out_specs=(
+            moving,
+            pl.BlockSpec((state_count, channels, row_count // OUT_STEPS), lambda i: (0, 0, i)),
+            *small,
+        ),
         compiler_params=pltpu.CompilerParams(vmem_limit_bytes=VMEM_LIMIT),
     )(layer, mixed_grad, grad_weight, grad_bias, grad_depth, depth_weight)
     return layer_out, grad_states, grad_weight, grad_bias[0], grad_depth

time: 43 us -> 44 us (1.023)
  Pallas kernels: 41.5 us -> 42.5 us
    pallas_call x1, Pallas kernels: 2.35 us -> 3.56 us  [local(): pl.pallas_call(output_kernel, out_shape=(jax.ShapeDtypeStruct((channels,...]
where the time goes in v6:
time: 44 us; the launch traced here: 43.8 us
  Pallas kernels  42.5 us (97%)
  between operations  1.29 us (3%)
    pallas_call x1, Pallas kernels, local(): pl.pallas_call(functools.partial(whole_kernel, (vert, feat, channels, row...  38.9 us
    pallas_call x1, Pallas kernels, local(): pl.pallas_call(output_kernel, out_shape=(jax.ShapeDtypeStruct((channels,...  3.56 us

profile of v6, /device:TPU:0, one launch (start us, length us, event | category | flops | bytes accessed | tf_op | source)
XLA Modules:
  0.0 43.8 jit_solution(2972646113384730152)
XLA Ops:
  1.3 38.9 %shard_map.137 = (bf16[32,4096]{1,0:T(8,128)(2,1)}, f32[32,4096]{1,0:T(8,128)}, f32[32,256]{1,0:T(8,128)}, f32[1,32]{1,0:T(1,128)}, f32[4,32]{1,0:T(4,128)}) custom-call(s32[1]{0:T(128)S(6)} %copy.15.count_ref, s32[1,256]{1,0:T(1,128)} %dst_ref.1, s32[1,256]{1,0:T(1,128)} %src_ref.1, f32[4,32]{1,0:T(4,128)} %depth_ref.3, s32[1,4,64]{2,1,0:T(4,128)} %rows_ref.1, ...), custom_call_target="tpu_custom_call" | custom-call | tf_op jit(solution)/shard_map/pallas_call | solution.py:570
  40.2 3.6 %shard_map.138 = (bf16[32,4096]{1,0:T(8,128)(2,1)}, bf16[4,32,4096]{2,1,0:T(8,128)(2,1)}, f32[32,256]{1,0:T(8,128)}, f32[1,32]{1,0:T(1,128)}, f32[4,32]{1,0:T(4,128)}) custom-call(bf16[32,4096]{1,0:T(8,128)(2,1)} %get-tuple-element.15.layer, f32[32,4096]{1,0:T(8,128)} %get-tuple-element.16.mixed_grad, f32[32,256]{1,0:T(8,128)} %get-tuple-element.17.grad_weight, ...), custom_call_target="tpu_custom_call" | custom-call | tf_op jit(solution)/shard_map/pallas_call | solution.py:640

commit v7 on v6

--- a/solution.py
+++ b/solution.py
@@ -13,7 +13,6 @@
 HALO_OUT, COT, BIAS, LAYER, TERMS, HALO_BACK, SUMS, DEPTH, AGG, AGG_B, GRAD, GRAD_B = range(12)
 TILE_PARTS = 8
 GROUP = 10
-OUT_STEPS = 4
 REPEAT = 3
 VMEM_LIMIT = 63 * 1024 * 1024
 STRIDE = 128
@@ -631,12 +630,6 @@
         cotangent,
         tile_values,
     )
-
-    def still(shape):
-        return pl.BlockSpec(shape, lambda i: (0, 0))
-
-    moving = pl.BlockSpec((channels, row_count // OUT_STEPS), lambda i: (0, i))
-    small = [still((channels, features)), still((1, channels)), still((state_count, channels))]
     layer_out, grad_states, grad_weight, grad_bias, grad_depth = pl.pallas_call(
         output_kernel,
         out_shape=(
@@ -646,13 +639,8 @@
             jax.ShapeDtypeStruct((1, channels), F32),
             jax.ShapeDtypeStruct((state_count, channels), F32),
         ),
-        grid=(OUT_STEPS,),
-        in_specs=[moving, moving, *small, still(depth_weight.shape)],
-        out_specs=(
-            moving,
-            pl.BlockSpec((state_count, channels, row_count // OUT_STEPS), lambda i: (0, 0, i)),
-            *small,
-        ),
+        in_specs=[vmem] * 6,
+        out_specs=(vmem,) * 5,
         compiler_params=pltpu.CompilerParams(vmem_limit_bytes=VMEM_LIMIT),
     )(layer, mixed_grad, grad_weight, grad_bias, grad_depth, depth_weight)
     return layer_out, grad_states, grad_weight, grad_bias[0], grad_depth

time: 44 us -> 42.7 us (0.970)
  Pallas kernels: 42.5 us -> 41.3 us
    pallas_call x1, Pallas kernels: 3.56 us -> 2.35 us  [local(): pl.pallas_call(output_kernel, out_shape=(jax.ShapeDtypeStruct((channels,...]
where the time goes in v7:
time: 42.7 us; the launch traced here: 42.6 us
  Pallas kernels  41.3 us (97%)
  between operations  1.29 us (3%)
    pallas_call x1, Pallas kernels, local(): pl.pallas_call(functools.partial(whole_kernel, (vert, feat, channels, row...  38.9 us
    pallas_call x1, Pallas kernels, local(): pl.pallas_call(output_kernel, out_shape=(jax.ShapeDtypeStruct((channels,...  2.35 us

profile of v7, /device:TPU:0, one launch (start us, length us, event | category | flops | bytes accessed | tf_op | source)
XLA Modules:
  0.0 42.6 jit_solution(8985743290659571067)
XLA Ops:
  1.3 38.9 %shard_map.137 = (bf16[32,4096]{1,0:T(8,128)(2,1)}, f32[32,4096]{1,0:T(8,128)}, f32[32,256]{1,0:T(8,128)}, f32[1,32]{1,0:T(1,128)}, f32[4,32]{1,0:T(4,128)}) custom-call(s32[1]{0:T(128)S(6)} %copy.15.count_ref, s32[1,256]{1,0:T(1,128)} %dst_ref.1, s32[1,256]{1,0:T(1,128)} %src_ref.1, f32[4,32]{1,0:T(4,128)} %depth_ref.3, s32[1,4,64]{2,1,0:T(4,128)} %rows_ref.1, ...), custom_call_target="tpu_custom_call" | custom-call | tf_op jit(solution)/shard_map/pallas_call | solution.py:569
  40.2 2.4 %shard_map.138 = (bf16[32,4096]{1,0:T(8,128)(2,1)}, bf16[4,32,4096]{2,1,0:T(8,128)(2,1)}, f32[32,256]{1,0:T(8,128)}, f32[1,32]{1,0:T(1,128)}, f32[4,32]{1,0:T(4,128)}) custom-call(bf16[32,4096]{1,0:T(8,128)(2,1)} %get-tuple-element.15.layer, f32[32,4096]{1,0:T(8,128)} %get-tuple-element.16.mixed_grad, f32[32,256]{1,0:T(8,128)} %get-tuple-element.17.grad_weight, ...), custom_call_target="tpu_custom_call" | custom-call | tf_op jit(solution)/shard_map/pallas_call | solution.py:633
